TPU v7x, 128 devices: a whole 4x4x4 slice. The times are simulated.
128 devices in a mesh: sector: 16 (over z, x), mpo: 8 (over y, core).
Axes of the slice: x: 4, y: 4, z: 4, core: 2. Of those that a mesh axis runs over, the one named last changes fastest.
Arguments:
- psi: float32 [16, 768, 768], P('sector'), may hold values from -24 to 24, as said below
- left_env: float32 [8, 16, 768, 768], P('mpo', 'sector'), may hold values from -0.21875 to 0.21875
- right_env: float32 [8, 16, 768, 768], P('mpo', 'sector'), may hold values from -0.21875 to 0.21875
- sector_label: int32 [16], replicated, may hold values from 0 to 15, as said below
- charge_step: int32 [8, 16, 3], replicated, may hold values from -1 to 1
- coef_index: int32 [8, 16, 3], replicated, may hold values from 0 to 7
- entry_values: float32 [8], replicated, may hold values from -1.5 to 1.5
- recurrence: float32 [3], replicated, may hold values from -2 to 2
Outputs:
- vec_one: float32 [16, 768, 768], P('sector')
- vec_two: float32 [16, 768, 768], P('sector')
Inputs may be any that keep to these rules, and one draw needn't show every extreme that they name: `psi`: each sector block's entries lie in this range. `sector_label`: A permutation of the labels over the slots; two sectors whose labels differ by one lie at most 3 slots apart.
All inputs are finite; a program needn't handle non-finite values.
Results may differ from a plain program's by a relative error of at most 0.0029.
Values may be sent and summed in bfloat16 or wider, within the bound.
No kernel may reach another device: no remote copies, remote signals or barrier semaphores. Data moves between devices by JAX's collectives and lax.ppermute only.
A program may use at most 64 MiB of HBM per device.

v0:
```python
import functools

import jax
import jax.numpy as jnp
from jax import lax
from jax.experimental import pallas as pl
from jax.experimental.pallas import tpu as pltpu
from jax.sharding import PartitionSpec as P

EPS = 1e-06
SIDE = 4
CHUNKS = 2
LATE = True
WHEN = 1
ENV = 0.21875
F16_TOP = 60000.0
TILE = 16
NOTE = 130.0
F32, BF16, F16 = jnp.float32, jnp.bfloat16, jnp.float16
VMEM_LIMIT = 16 * 1024 * 1024
in_vmem = pl.BlockSpec(memory_space=pltpu.VMEM)
in_smem = pl.BlockSpec(memory_space=pltpu.SMEM)


def along_x(block, step):
    route = [
        (SIDE * z + x, SIDE * z + (x + step) % SIDE) for z in range(SIDE) for x in range(SIDE)
    ]
    return lax.ppermute(block, "sector", route)


def along_z(block, step):
    count = SIDE * SIDE
    route = [(i, i + SIDE * step) for i in range(count) if 0 <= i + SIDE * step < count]
    return lax.ppermute(block, "sector", route)


def around_z(block, step):
    count = SIDE * SIDE
    return lax.ppermute(
        block, "sector", [(i, (i + SIDE * step) % count) for i in range(count)]
    )


def along_y(block, step):
    route = [
        (2 * y + core, 2 * ((y + step) % SIDE) + core) for y in range(SIDE) for core in range(2)
    ]
    return lax.ppermute(block, "mpo", route)


def other_core(block):
    return lax.ppermute(block, "mpo", [(i, i ^ 1) for i in range(2 * SIDE)])


def pick(array, index):
    return lax.dynamic_index_in_dim(array, index, 0, keepdims=False)


def after(value, earlier):
    return lax.optimization_barrier((value, earlier))[0]


def call(body, outs, smem, vmem, scratch=(), flops=0):
    shapes = [jax.ShapeDtypeStruct(shape, dtype) for shape, dtype in outs]
    moved = sum(a.size * a.dtype.itemsize for a in vmem)
    moved += sum(s.size * s.dtype.itemsize for s in shapes)
    return pl.pallas_call(
        body,
        out_shape=shapes,
        in_specs=[in_smem] * len(smem) + [in_vmem] * len(vmem),
        out_specs=[in_vmem] * len(outs),
        scratch_shapes=list(scratch),
        compiler_params=pltpu.CompilerParams(vmem_limit_bytes=VMEM_LIMIT),
        cost_estimate=pl.CostEstimate(flops=flops, bytes_accessed=moved, transcendentals=0),
    )(*smem, *vmem)


def halves_of(array):
    head = array.astype(BF16)
    return head, (array - head.astype(F32)).astype(BF16)


def dot(a, b):
    return jnp.dot(a, b, preferred_element_type=F32)


def product_kernel(row, noted, place, left, vector, squares, *refs):
    outs, acc = refs[:SIDE], refs[-1]
    rows, m = acc.shape
    part = rows // SIDE
    left_head, left_tail = halves_of(left[pl.ds(row, rows), :])
    wide = m // 3
    for n in range(3):
        cols = slice(n * wide, (n + 1) * wide)
        head, tail = halves_of(vector[:, cols])
        acc[:, cols] = dot(left_head, head) + (dot(left_head, tail) + dot(left_tail, head))
    x = place[0]
    if noted:
        power = jnp.ceil(0.5 * jnp.log2(jnp.clip(squares[...], 1e-36, 1e36)) + 0.01)
        note = jnp.broadcast_to(power[:1, :1] + NOTE, (TILE, m)).astype(BF16)
    for d in range(SIDE):
        start = pl.multiple_of(lax.rem(x + d, SIDE) * part, part)
        outs[d][:part, :] = acc[pl.ds(start, part), :].astype(BF16)
        if noted:
            outs[d][part:, :] = note


def squares_kernel(vector, out):
    rows, m = vector.shape
    step_rows = 64

    def step(i, total):
        value = vector[pl.ds(pl.multiple_of(i * step_rows, step_rows), step_rows), :]
        return total + jnp.sum((value * value).reshape(-1, 8, m), axis=0)

    total = lax.fori_loop(0, rows // step_rows, step, jnp.zeros((8, m), F32))
    out[...] = jnp.full(out.shape, jnp.sum(total), F32)


def select_kernel(part, skips, *refs):
    near, outs = refs[:SIDE], refs[SIDE:]
    for skip, out in ((skips[0], outs[0]), (skips[1], outs[1])):
        for e in range(SIDE):
            at = jnp.where(skip < e, e - 1, min(e, SIDE - 2)) * part

            @pl.when(skip != e)
            def _():
                out[pl.ds(pl.multiple_of(at, part), part), :] = near[e][:part, :]

        if near[0].shape[0] > part:
            notes = [n[part:, :].astype(F32) for n in near]
            out[(SIDE - 1) * part :, :] = functools.reduce(jnp.maximum, notes).astype(BF16)


def mix_kernel(noted, weight, scale, *refs):
    near, up, down = refs[:SIDE], refs[SIDE], refs[SIDE + 1]
    if noted:
        out, note = refs[SIDE + 2 :]
        part = out.shape[1]
        notes = [n[part:, :].astype(F32) for n in near]
        notes += [n[(SIDE - 1) * part :, :].astype(F32) for n in (up, down)]
        note[...] = functools.reduce(jnp.maximum, notes)
    else:
        note, out = refs[SIDE + 2 :]
        part = out.shape[1]
    factor = jnp.exp2(NOTE - note[...]) * scale[0]

    def step(i, carry):
        def at(piece):
            return pl.ds(pl.multiple_of(piece * part + i * TILE, TILE), TILE)

        blocks = [near[j][at(0), :] for j in range(SIDE)]
        blocks += [up[at(j), :] for j in range(SIDE - 1)] + [down[at(j), :] for j in range(SIDE - 1)]
        sums = [None] * SIDE
        for j, block in enumerate(blocks):
            block = block.astype(F32)
            for d in range(SIDE):
                term = block * weight[d * 10 + j]
                sums[d] = term if j == 0 else sums[d] + term
        for d in range(SIDE):
            out[d, at(0), :] = sums[d] * factor
        return carry

    lax.fori_loop(0, part // TILE, step, 0)


def term_kernel(place, scale, mixed, right, mine, theirs, acc):
    eighth = mine.shape[1]
    half = SIDE * eighth
    left_head, left_tail = halves_of(mixed[...])
    wide = acc.shape[1] // 3
    for n in range(3):
        cols = slice(n * wide, (n + 1) * wide)
        head, tail = halves_of(right[:, cols])
        acc[:, cols] = dot(left_head, head) + (dot(left_head, tail) + dot(left_tail, head))
    y, core, factor = place[1], place[2], scale[0]
    for e in range(SIDE):
        quarter = lax.rem(y + e, SIDE) * eighth
        for out, side in ((mine, core), (theirs, 1 - core)):
            start = pl.multiple_of(side * half + quarter, eighth)
            out[e] = acc[pl.ds(start, eighth), :] * factor


def assemble_kernel(place, scale, mine, theirs, out, stats):
    chunks, eighth, m = mine.shape[1:]
    part = 2 * eighth
    x, y, core = place[0], place[1], place[2]
    squares = jnp.zeros((8, m), F32)
    for c in range(chunks):
        for block, side in ((mine, core), (theirs, 1 - core)):
            for e in range(SIDE):
                quarter = lax.rem(y - e + SIDE, SIDE)
                k = lax.rem(x - 2 * side - quarter // 2 + SIDE, SIDE)
                start = c * SIDE * part + k * part + lax.rem(quarter, 2) * eighth
                value = block[e, c] * scale[0]
                out[pl.ds(pl.multiple_of(start, eighth), eighth), :] = value
                squares = squares + jnp.sum((value * value).reshape(-1, 8, m), axis=0)
    stats[...] = jnp.full(stats.shape, jnp.sum(squares), F32)


def combined(tiles):
    return functools.reduce(jnp.add, tiles)


def of_line(tile):
    return combined([tile] + [along_x(tile, d) for d in range(1, SIDE)])


def of_lines(line):
    return combined([line] + [around_z(line, d) for d in range(1, SIDE)])


def local(
    psi, left_env, right_env, sector_label, charge_step, coef_index, entry_values, recurrence
):
    slot = lax.axis_index("sector")
    bond = lax.axis_index("mpo")
    z, x = slot // SIDE, slot % SIDE
    y, core = bond // 2, bond % 2
    place = jnp.stack([x, y, core]).astype(jnp.int32)
    psi, left, right = psi[0], left_env[0, 0], right_env[0, 0]
    m = psi.shape[0]
    slots = sector_label.shape[0]
    cells = float(slots * m * m)
    rows = m // CHUNKS
    part = rows // SIDE
    half = rows // 2
    eighth = half // SIDE
    flops = 6 * rows * m * m

    ds = jnp.arange(SIDE, dtype=jnp.int32)
    three = ds[: SIDE - 1]
    skip_up, skip_down = x, (x + 1) % SIDE
    skips = jnp.stack([skip_up, skip_down]).astype(jnp.int32)
    up_d = three + (three >= skip_up)
    down_d = three + (three >= skip_down)
    goal = SIDE * z + (x + ds) % SIDE
    source = jnp.concatenate(
        [
            SIDE * z + (x - ds) % SIDE,
            SIDE * (z - 1) + (x - up_d) % SIDE,
            SIDE * (z + 1) + (x - down_d) % SIDE,
        ]
    )

    table = jnp.arange(entry_values.shape[0], dtype=jnp.int32)
    every = jnp.arange(slots, dtype=jnp.int32)
    step_bond, index_bond = pick(charge_step, bond), pick(coef_index, bond)
    values = jnp.sum(jnp.where(index_bond[..., None] == table, entry_values, F32(0.0)), axis=-1)
    target = sector_label[:, None] + step_bond
    goal_label = jnp.sum(jnp.where(goal[:, None] == every, sector_label, 0), axis=1)
    into = jnp.sum(
        jnp.where(target[None] == goal_label[:, None, None], values[None], F32(0.0)), axis=2
    )
    weight = jnp.sum(
        jnp.where(source[None, :, None] == every, into[:, None, :], F32(0.0)), axis=2
    ).reshape(-1)

    def spread(pieces):
        return [pieces[0]] + [along_x(pieces[d], d) for d in range(1, SIDE)]

    def next_rows(near, earlier):
        noted = near[0].shape[0] > part
        out = (((SIDE - 1) * part + TILE * noted, m), BF16)
        up, down = call(functools.partial(select_kernel, part), [out] * 2, [skips], near)
        up, down = after((up, down), earlier)
        return [along_z(up, 1), along_z(down, -1)]

    def mix(near, beyond, note, weights):
        noted = near[0].shape[0] > part
        out, note_out = ((SIDE, part, m), F32), ((TILE, m), F32)
        got = call(
            functools.partial(mix_kernel, noted),
            [out] + [note_out] * noted,
            [weights, z_scale.reshape(1)],
            near + beyond + ([] if noted else [note]),
            flops=80 * part * m,
        )
        sums = got[0].astype(F16)
        mixed = jnp.concatenate([sums[0]] + [along_x(sums[d], d) for d in range(1, SIDE)])
        return mixed, got[1] if noted else note

    def reduce_bonds(mixed, scale):
        chips = []
        for c in range(CHUNKS):
            mine, theirs = call(
                term_kernel,
                [((SIDE, eighth, m), F32)] * 2,
                [place, scale.reshape(1)],
                [mixed[c].astype(F32), right],
                [pltpu.VMEM((rows, m), F32)],
                flops,
            )
            chips.append(mine + other_core(theirs.astype(F16)).astype(F32))
        chip = jnp.stack(chips, 1)
        sent = chip.astype(F16)
        total = chip[0]
        for e in range(1, SIDE):
            total = total + along_y(sent[e], e).astype(F32)
        return total

    def share_bonds(piece, factor):
        mine = jnp.stack([piece] + [along_y(piece, e) for e in range(1, SIDE)])
        return call(
            assemble_kernel,
            [((m, m), F32), ((8, 128), F32)],
            [place, factor.reshape(1)],
            [mine.astype(F32), other_core(mine).astype(F32)],
        )

    def own_rows(array):
        k = (x - 2 * core - y // 2) % SIDE
        start = k * part + (y % 2) * eighth
        return lax.dynamic_slice_in_dim(array.reshape(CHUNKS, rows, m), start, eighth, 1)

    def products(chunk, vector, squares):
        noted = chunk == 0
        return call(
            functools.partial(product_kernel, chunk * rows, noted),
            [((part + TILE * noted, m), BF16)] * SIDE,
            [place],
            [left, vector, squares],
            [pltpu.VMEM((rows, m), F32)],
            flops,
        )

    def hamiltonian(vector, squares, summed):
        pieces = [products(c, vector, squares) for c in range(CHUNKS)]
        near, beyond, mixed, note, total = [], [], [], None, squares
        for p in pieces:
            near.append(after(spread(after(p, near[-1:])), pieces[-1][0]))
        scaled = weight
        if summed:
            line = of_line(after(squares, pieces[-1][0]))
            if LATE:
                near[-1] = after(near[-1], line)
        for p in near:
            beyond.append(next_rows(p, beyond[-1:]))
        if summed:
            total = of_lines(line)
        for c in range(CHUNKS):
            if summed and c == WHEN:
                scaled = after(scaled, total)
            rows_mixed, note = mix(near[c], beyond[c], note, scaled)
            mixed.append(rows_mixed)
        power = jnp.exp2(note[0, 0] - NOTE)
        return reduce_bonds(mixed, h_scale / z_scale), power, total

    reach = ENV * m**0.5
    spread_of = 9.0 * jnp.max(jnp.abs(entry_values)) + F32(1e-30)
    z_scale = F16_TOP / (1.02 * reach * spread_of)
    h_scale = F16_TOP / (8.4 * reach * reach * spread_of)
    small = F32(1e-18)

    squares = call(squares_kernel, [((8, 128), F32)], [], [psi])[0]
    psi_norm = jnp.sqrt(squares[0, 0]) + small
    piece, power, _ = hamiltonian(psi, squares, False)
    bound = F16_TOP / (1.05 * (power * (F16_TOP / h_scale) + 2.0 * psi_norm))
    piece = piece * (power * (bound / h_scale)) - (bound * recurrence[0]) * own_rows(psi)
    resid, squares = share_bonds(piece.astype(F16), 1.0 / bound)

    piece, power, tile = hamiltonian(resid, squares, True)
    own_norm = jnp.sqrt(squares[0, 0]) + small
    gain = 1.0 / jnp.sqrt(tile[0, 0] / cells + EPS)
    vec_one = resid * gain
    bound = gain * (power * (F16_TOP / h_scale) + 2.0 * own_norm) + 2.0 * psi_norm
    bound = F16_TOP / (1.05 * bound)
    piece = piece * (power * gain * (bound / h_scale))
    piece = piece - (bound * gain * recurrence[1]) * own_rows(resid)
    piece = piece - (bound * recurrence[2]) * own_rows(psi)
    resid, squares = share_bonds(piece.astype(F16), 1.0 / bound)
    mean = of_lines(of_line(squares))[0, 0] / cells
    vec_two = resid * (1.0 / jnp.sqrt(mean + EPS))
    return (vec_one[None], vec_two[None])


def solution(mesh):
    in_specs = (
        P("sector", None, None),
        P("mpo", "sector", None, None),
        P("mpo", "sector", None, None),
        P(),
        P(),
        P(),
        P(),
        P(),
    )
    out_specs = (P("sector", None, None), P("sector", None, None))
    return jax.shard_map(local, mesh=mesh, in_specs=in_specs, out_specs=out_specs, check_vma=False)
```

profile of v0, /device:TPU:1, one launch (start us, length us, event | category | flops | bytes accessed | tf_op | source)
XLA Modules:
  0.0 216.2 jit_solution(9512464144419473196)
XLA Ops:
  5.7 2.9 %shard_map.96 = (bf16[112,768]{1,0:T(8,128)(2,1)S(1)}, bf16[112,768]{1,0:T(8,128)(2,1)}, bf16[112,768]{1,0:T(8,128)(2,1)S(1)}, bf16[112,768]{1,0:T(8,128)(2,1)S(1)}) custom-call(s32[3]{0:T(128)S(1)} %get-tuple-element.183.place, f32[768,768]{1,0:T(8,128)S(1)} %bitcast.128, f32[768,768]{1,0:T(8,128)S(1)} %bitcast.123, f32[8,128]{1,0:T(8,128)S(1)} %shard_map.95.squares), custom_call_target="tpu_custom_call" | custom-call | flops 1358954496 | bytes 5410816 | tf_op jit(solution)/shard_map/pallas_call | solution.py:68
  10.6 2.4 %collective-permute-start.1 = (bf16[112,768]{1,0:T(8,128)(2,1)S(1)}, bf16[112,768]{1,0:T(8,128)(2,1)S(1)}, u32[]{:S(2)}, u32[]{:S(2)}) collective-permute-start(bf16[112,768]{1,0:T(8,128)(2,1)S(1)} %get-tuple-element.78), channel_id=1, source_target_pairs={{0,16},{8,24},{16,0},{24,8},{32,48},{40,56},{48,32},{56,40},{64,80... | collective-permute-start | bytes 516104 | tf_op jit(solution)/shard_map/ppermute | solution.py:29
  22.3 4.3 %collective-permute-start.3 = (bf16[304,768]{1,0:T(8,128)(2,1)}, bf16[304,768]{1,0:T(8,128)(2,1)}, u32[]{:S(2)}, u32[]{:S(2)}) collective-permute-start(bf16[304,768]{1,0:T(8,128)(2,1)} %get-tuple-element.85), channel_id=1, source_target_pairs={{0,32},{8,40},{16,48},{24,56},{32,64},{40,72},{48,80},{56,88},{64,... | collective-permute-start | bytes 1400840 | tf_op jit(solution)/shard_map/ppermute | solution.py:35
  39.8 4.5 %collective-permute-start.12 = (bf16[288,768]{1,0:T(8,128)(2,1)}, bf16[288,768]{1,0:T(8,128)(2,1)}, u32[]{:S(2)}, u32[]{:S(2)}) collective-permute-start(bf16[288,768]{1,0:T(8,128)(2,1)} %get-tuple-element.104), channel_id=1, source_target_pairs={{0,32},{8,40},{16,48},{24,56},{32,64},{40,72},{48,80},{56,88},{64,... | collective-permute-start | bytes 1327112 | tf_op jit(solution)/shard_map/ppermute | solution.py:35
  51.3 3.7 %collective-permute-done.13.refs_5_ = bf16[288,768]{1,0:T(8,128)(2,1)} collective-permute-done((bf16[288,768]{1,0:T(8,128)(2,1)}, bf16[288,768]{1,0:T(8,128)(2,1)}, u32[]{:S(2)}, u32[]{:S(2)}) %collective-permute-start.13) | collective-permute-done | bytes 442400 | tf_op jit(solution)/shard_map/ppermute | solution.py:35
  62.9 4.9 %collective-permute-start.8 = (f16[4,48,768]{2,1,0:T(8,128)(2,1)S(1)}, f16[4,48,768]{2,1,0:T(8,128)(2,1)S(1)}, u32[]{:S(2)}, u32[]{:S(2)}) collective-permute-start(f16[4,48,768]{2,1,0:T(8,128)(2,1)S(1)} %convert_element_type.100), channel_id=1, source_target_pairs={{0,1},{1,0},{2,3},{3,2},{4,5},{5,4},{6,7},{7,6},{8,9},{9,8},{10,11... | collective-permute-start | bytes 884744 | tf_op jit(solution)/shard_map/ppermute | solution.py:53
  70.2 4.4 %collective-permute-start.17 = (f16[4,48,768]{2,1,0:T(8,128)(2,1)S(1)}, f16[4,48,768]{2,1,0:T(8,128)(2,1)S(1)}, u32[]{:S(2)}, u32[]{:S(2)}) collective-permute-start(f16[4,48,768]{2,1,0:T(8,128)(2,1)S(1)} %convert_element_type.104), channel_id=1, source_target_pairs={{0,1},{1,0},{2,3},{3,2},{4,5},{5,4},{6,7},{7,6},{8,9},{9,8},{10,11... | collective-permute-start | bytes 884744 | tf_op jit(solution)/shard_map/ppermute | solution.py:53
  85.0 2.7 %collective-permute-done.19 = f16[2,48,768]{2,1,0:T(8,128)(2,1)S(1)} collective-permute-done((f16[2,48,768]{2,1,0:T(8,128)(2,1)}, f16[2,48,768]{2,1,0:T(8,128)(2,1)S(1)}, u32[]{:S(2)}, u32[]{:S(2)}) %collective-permute-start.19) | collective-permute-done | bytes 147488 | tf_op jit(solution)/shard_map/ppermute | solution.py:49
  92.8 2.5 %collective-permute-done.22 = f16[2,48,768]{2,1,0:T(8,128)(2,1)S(1)} collective-permute-done((f16[2,48,768]{2,1,0:T(8,128)(2,1)S(1)}, f16[2,48,768]{2,1,0:T(8,128)(2,1)S(1)}, u32[]{:S(2)}, u32[]{:S(2)}) %collective-permute-start.22) | collective-permute-done | bytes 147488 | tf_op jit(solution)/shard_map/ppermute | solution.py:49
  95.2 2.4 %collective-permute-done.21 = f16[2,48,768]{2,1,0:T(8,128)(2,1)S(1)} collective-permute-done((f16[2,48,768]{2,1,0:T(8,128)(2,1)S(1)}, f16[2,48,768]{2,1,0:T(8,128)(2,1)S(1)}, u32[]{:S(2)}, u32[]{:S(2)}) %collective-permute-start.21) | collective-permute-done | bytes 147488 | tf_op jit(solution)/shard_map/ppermute | solution.py:49
  98.7 3.0 %collective-permute-start.24 = (f16[4,2,48,768]{3,2,1,0:T(8,128)(2,1)}, f16[4,2,48,768]{3,2,1,0:T(8,128)(2,1)}, u32[]{:S(2)}, u32[]{:S(2)}) collective-permute-start(f16[4,2,48,768]{3,2,1,0:T(8,128)(2,1)} %get-tuple-element.163), channel_id=1, source_target_pairs={{0,1},{1,0},{2,3},{3,2},{4,5},{5,4},{6,7},{7,6},{8,9},{9,8},{10,11... | collective-permute-start | bytes 1769480 | tf_op jit(solution)/shard_map/ppermute | solution.py:53
  106.4 2.3 %shard_map.106 = (bf16[112,768]{1,0:T(8,128)(2,1)S(1)}, bf16[112,768]{1,0:T(8,128)(2,1)S(1)}, bf16[112,768]{1,0:T(8,128)(2,1)S(1)}, bf16[112,768]{1,0:T(8,128)(2,1)S(1)}) custom-call(s32[3]{0:T(128)S(1)} %get-tuple-element.183.place, f32[768,768]{1,0:T(8,128)S(1)} %bitcast.130, f32[768,768]{1,0:T(8,128)S(1)} %get-tuple-element.108.vector, ...), custom_call_target="tpu_custom_call" | custom-call | flops 1358954496 | bytes 5410816 | tf_op jit(solution)/shard_map/pallas_call | solution.py:68
  113.8 5.5 %collective-permute-done.31.refs_1_ = bf16[112,768]{1,0:T(8,128)(2,1)S(1)} collective-permute-done((bf16[112,768]{1,0:T(8,128)(2,1)S(1)}, bf16[112,768]{1,0:T(8,128)(2,1)S(1)}, u32[]{:S(2)}, u32[]{:S(2)}) %collective-permute-start.31) | collective-permute-done | bytes 172064 | tf_op jit(solution)/shard_map/ppermute | solution.py:29
  120.4 2.6 %collective-permute-start.34 = (bf16[304,768]{1,0:T(8,128)(2,1)S(1)}, bf16[304,768]{1,0:T(8,128)(2,1)S(1)}, u32[]{:S(2)}, u32[]{:S(2)}) collective-permute-start(bf16[304,768]{1,0:T(8,128)(2,1)S(1)} %get-tuple-element.120), channel_id=1, source_target_pairs={{0,32},{8,40},{16,48},{24,56},{32,64},{40,72},{48,80},{56,88},{64,... | collective-permute-start | bytes 1400840 | tf_op jit(solution)/shard_map/ppermute | solution.py:35
  124.3 2.8 %collective-permute-start.27 = (f32[8,128]{1,0:T(8,128)S(1)}, f32[8,128]{1,0:T(8,128)S(1)}, u32[]{:S(2)}, u32[]{:S(2)}) collective-permute-start(f32[8,128]{1,0:T(8,128)S(1)} %get-tuple-element.111.squares), channel_id=1, source_target_pairs={{0,24},{8,0},{16,8},{24,16},{32,56},{40,32},{48,40},{56,48},{64,88... | collective-permute-start | bytes 12296 | tf_op jit(solution)/shard_map/ppermute | solution.py:29
  133.4 3.6 %collective-permute-start.30 = (f32[8,128]{1,0:T(8,128)S(1)}, f32[8,128]{1,0:T(8,128)S(1)}, u32[]{:S(2)}, u32[]{:S(2)}) collective-permute-start(f32[8,128]{1,0:T(8,128)S(1)} %add_add_fusion.3), channel_id=1, source_target_pairs={{0,96},{8,104},{16,112},{24,120},{32,0},{40,8},{48,16},{56,24},{64... | collective-permute-start | bytes 12296 | tf_op jit(solution)/shard_map/ppermute | solution.py:40
  137.6 3.5 %collective-permute-start.29 = (f32[8,128]{1,0:T(8,128)S(1)}, f32[8,128]{1,0:T(8,128)S(1)}, u32[]{:S(2)}, u32[]{:S(2)}) collective-permute-start(f32[8,128]{1,0:T(8,128)S(1)} %add_add_fusion.3), channel_id=1, source_target_pairs={{0,64},{8,72},{16,80},{24,88},{32,96},{40,104},{48,112},{56,120},{... | collective-permute-start | bytes 12296 | tf_op jit(solution)/shard_map/ppermute | solution.py:40
  151.0 3.7 %collective-permute-done.44.refs_5_ = bf16[288,768]{1,0:T(8,128)(2,1)S(1)} collective-permute-done((bf16[288,768]{1,0:T(8,128)(2,1)S(1)}, bf16[288,768]{1,0:T(8,128)(2,1)S(1)}, u32[]{:S(2)}, u32[]{:S(2)}) %collective-permute-start.44) | collective-permute-done | bytes 442400 | tf_op jit(solution)/shard_map/ppermute | solution.py:35
  161.1 5.1 %collective-permute-start.39 = (f16[4,48,768]{2,1,0:T(8,128)(2,1)S(1)}, f16[4,48,768]{2,1,0:T(8,128)(2,1)S(1)}, u32[]{:S(2)}, u32[]{:S(2)}) collective-permute-start(f16[4,48,768]{2,1,0:T(8,128)(2,1)S(1)} %convert_element_type.115), channel_id=1, source_target_pairs={{0,1},{1,0},{2,3},{3,2},{4,5},{5,4},{6,7},{7,6},{8,9},{9,8},{10,11... | collective-permute-start | bytes 884744 | tf_op jit(solution)/shard_map/ppermute | solution.py:53
  168.7 3.5 %collective-permute-start.48 = (f16[4,48,768]{2,1,0:T(8,128)(2,1)S(1)}, f16[4,48,768]{2,1,0:T(8,128)(2,1)S(1)}, u32[]{:S(2)}, u32[]{:S(2)}) collective-permute-start(f16[4,48,768]{2,1,0:T(8,128)(2,1)S(1)} %convert_element_type.119), channel_id=1, source_target_pairs={{0,1},{1,0},{2,3},{3,2},{4,5},{5,4},{6,7},{7,6},{8,9},{9,8},{10,11... | collective-permute-start | bytes 884744 | tf_op jit(solution)/shard_map/ppermute | solution.py:53
  174.3 2.7 %collective-permute-start.51 = (f16[2,48,768]{2,1,0:T(8,128)(2,1)}, f16[2,48,768]{2,1,0:T(8,128)(2,1)}, u32[]{:S(2)}, u32[]{:S(2)}) collective-permute-start(f16[2,48,768]{2,1,0:T(8,128)(2,1)} %get-tuple-element.153), channel_id=1, source_target_pairs={{0,6},{1,7},{2,0},{3,1},{4,2},{5,3},{6,4},{7,5},{8,14},{9,15},{10,... | collective-permute-start | bytes 442376 | tf_op jit(solution)/shard_map/ppermute | solution.py:49
  184.6 3.4 %collective-permute-start.54 = (f16[2,48,768]{2,1,0:T(8,128)(2,1)S(1)}, f16[2,48,768]{2,1,0:T(8,128)(2,1)S(1)}, u32[]{:S(2)}, u32[]{:S(2)}) collective-permute-start(f16[2,48,768]{2,1,0:T(8,128)(2,1)S(1)} %fusion.10), channel_id=1, source_target_pairs={{0,6},{1,7},{2,0},{3,1},{4,2},{5,3},{6,4},{7,5},{8,14},{9,15},{10,... | collective-permute-start | bytes 442376 | tf_op jit(solution)/shard_map/ppermute | solution.py:49
  188.7 3.0 %collective-permute-done.54 = f16[2,48,768]{2,1,0:T(8,128)(2,1)S(1)} collective-permute-done((f16[2,48,768]{2,1,0:T(8,128)(2,1)S(1)}, f16[2,48,768]{2,1,0:T(8,128)(2,1)S(1)}, u32[]{:S(2)}, u32[]{:S(2)}) %collective-permute-start.54) | collective-permute-done | bytes 147488 | tf_op jit(solution)/shard_map/ppermute | solution.py:49
  193.6 4.1 %collective-permute-done.52 = f16[2,48,768]{2,1,0:T(8,128)(2,1)S(1)} collective-permute-done((f16[2,48,768]{2,1,0:T(8,128)(2,1)S(1)}, f16[2,48,768]{2,1,0:T(8,128)(2,1)S(1)}, u32[]{:S(2)}, u32[]{:S(2)}) %collective-permute-start.52) | collective-permute-done | bytes 147488 | tf_op jit(solution)/shard_map/ppermute | solution.py:49
  (208 shorter events, 124.3 us)
Async XLA Ops:
  8.6 9.8 %collective-permute-start = (bf16[112,768]{1,0:T(8,128)(2,1)}, bf16[112,768]{1,0:T(8,128)(2,1)S(1)}, u32[]{:S(2)}, u32[]{:S(2)}) collective-permute-start(bf16[112,768]{1,0:T(8,128)(2,1)} %get-tuple-element.77), channel_id=1, source_target_pairs={{0,8},{8,16},{16,24},{24,0},{32,40},{40,48},{48,56},{56,32},{64,72... | collective-permute-start | bytes 516104 | tf_op jit(solution)/shard_map/ppermute | solution.py:29
  10.6 10.1 %collective-permute-start.1 = (bf16[112,768]{1,0:T(8,128)(2,1)S(1)}, bf16[112,768]{1,0:T(8,128)(2,1)S(1)}, u32[]{:S(2)}, u32[]{:S(2)}) collective-permute-start(bf16[112,768]{1,0:T(8,128)(2,1)S(1)} %get-tuple-element.78), channel_id=1, source_target_pairs={{0,16},{8,24},{16,0},{24,8},{32,48},{40,56},{48,32},{56,40},{64,80... | collective-permute-start | bytes 516104 | tf_op jit(solution)/shard_map/ppermute | solution.py:29
  22.3 17.5 %collective-permute-start.3 = (bf16[304,768]{1,0:T(8,128)(2,1)}, bf16[304,768]{1,0:T(8,128)(2,1)}, u32[]{:S(2)}, u32[]{:S(2)}) collective-permute-start(bf16[304,768]{1,0:T(8,128)(2,1)} %get-tuple-element.85), channel_id=1, source_target_pairs={{0,32},{8,40},{16,48},{24,56},{32,64},{40,72},{48,80},{56,88},{64,... | collective-permute-start | bytes 1400840 | tf_op jit(solution)/shard_map/ppermute | solution.py:35
  26.7 13.2 %collective-permute-start.4 = (bf16[304,768]{1,0:T(8,128)(2,1)}, bf16[304,768]{1,0:T(8,128)(2,1)}, u32[]{:S(2)}, u32[]{:S(2)}) collective-permute-start(bf16[304,768]{1,0:T(8,128)(2,1)} %get-tuple-element.86), channel_id=1, source_target_pairs={{32,0},{40,8},{48,16},{56,24},{64,32},{72,40},{80,48},{88,56},{96,... | collective-permute-start | bytes 1400840 | tf_op jit(solution)/shard_map/ppermute | solution.py:35
  39.8 11.5 %collective-permute-start.12 = (bf16[288,768]{1,0:T(8,128)(2,1)}, bf16[288,768]{1,0:T(8,128)(2,1)}, u32[]{:S(2)}, u32[]{:S(2)}) collective-permute-start(bf16[288,768]{1,0:T(8,128)(2,1)} %get-tuple-element.104), channel_id=1, source_target_pairs={{0,32},{8,40},{16,48},{24,56},{32,64},{40,72},{48,80},{56,88},{64,... | collective-permute-start | bytes 1327112 | tf_op jit(solution)/shard_map/ppermute | solution.py:35
  44.3 10.7 %collective-permute-start.13 = (bf16[288,768]{1,0:T(8,128)(2,1)}, bf16[288,768]{1,0:T(8,128)(2,1)}, u32[]{:S(2)}, u32[]{:S(2)}) collective-permute-start(bf16[288,768]{1,0:T(8,128)(2,1)} %get-tuple-element.105), channel_id=1, source_target_pairs={{32,0},{40,8},{48,16},{56,24},{64,32},{72,40},{80,48},{88,56},{96,... | collective-permute-start | bytes 1327112 | tf_op jit(solution)/shard_map/ppermute | solution.py:35
  48.4 11.3 %collective-permute-start.7 = (f16[96,768]{1,0:T(8,128)(2,1)S(1)}, f16[96,768]{1,0:T(8,128)(2,1)S(1)}, u32[]{:S(2)}, u32[]{:S(2)}) collective-permute-start(f16[96,768]{1,0:T(8,128)(2,1)S(1)} %get-tuple-element.173), channel_id=1, source_target_pairs={{0,24},{8,0},{16,8},{24,16},{32,56},{40,32},{48,40},{56,48},{64,88... | collective-permute-start | bytes 442376 | tf_op jit(solution)/shard_map/ppermute | solution.py:29
  50.3 10.2 %collective-permute-start.6 = (f16[96,768]{1,0:T(8,128)(2,1)S(1)}, f16[96,768]{1,0:T(8,128)(2,1)S(1)}, u32[]{:S(2)}, u32[]{:S(2)}) collective-permute-start(f16[96,768]{1,0:T(8,128)(2,1)S(1)} %get-tuple-element.174), channel_id=1, source_target_pairs={{0,16},{8,24},{16,0},{24,8},{32,48},{40,56},{48,32},{56,40},{64,80... | collective-permute-start | bytes 442376 | tf_op jit(solution)/shard_map/ppermute | solution.py:29
  50.8 9.7 %collective-permute-start.5 = (f16[96,768]{1,0:T(8,128)(2,1)S(1)}, f16[96,768]{1,0:T(8,128)(2,1)S(1)}, u32[]{:S(2)}, u32[]{:S(2)}) collective-permute-start(f16[96,768]{1,0:T(8,128)(2,1)S(1)} %get-tuple-element.175), channel_id=1, source_target_pairs={{0,8},{8,16},{16,24},{24,0},{32,40},{40,48},{48,56},{56,32},{64,72... | collective-permute-start | bytes 442376 | tf_op jit(solution)/shard_map/ppermute | solution.py:29
  57.4 10.4 %collective-permute-start.16 = (f16[96,768]{1,0:T(8,128)(2,1)S(1)}, f16[96,768]{1,0:T(8,128)(2,1)S(1)}, u32[]{:S(2)}, u32[]{:S(2)}) collective-permute-start(f16[96,768]{1,0:T(8,128)(2,1)S(1)} %get-tuple-element.169), channel_id=1, source_target_pairs={{0,24},{8,0},{16,8},{24,16},{32,56},{40,32},{48,40},{56,48},{64,88... | collective-permute-start | bytes 442376 | tf_op jit(solution)/shard_map/ppermute | solution.py:29
  62.9 11.7 %collective-permute-start.8 = (f16[4,48,768]{2,1,0:T(8,128)(2,1)S(1)}, f16[4,48,768]{2,1,0:T(8,128)(2,1)S(1)}, u32[]{:S(2)}, u32[]{:S(2)}) collective-permute-start(f16[4,48,768]{2,1,0:T(8,128)(2,1)S(1)} %convert_element_type.100), channel_id=1, source_target_pairs={{0,1},{1,0},{2,3},{3,2},{4,5},{5,4},{6,7},{7,6},{8,9},{9,8},{10,11... | collective-permute-start | bytes 884744 | tf_op jit(solution)/shard_map/ppermute | solution.py:53
  108.8 10.6 %collective-permute-start.31 = (bf16[112,768]{1,0:T(8,128)(2,1)S(1)}, bf16[112,768]{1,0:T(8,128)(2,1)S(1)}, u32[]{:S(2)}, u32[]{:S(2)}) collective-permute-start(bf16[112,768]{1,0:T(8,128)(2,1)S(1)} %get-tuple-element.113), channel_id=1, source_target_pairs={{0,8},{8,16},{16,24},{24,0},{32,40},{40,48},{48,56},{56,32},{64,72... | collective-permute-start | bytes 516104 | tf_op jit(solution)/shard_map/ppermute | solution.py:29
  108.9 10.5 %collective-permute-start.32 = (bf16[112,768]{1,0:T(8,128)(2,1)S(1)}, bf16[112,768]{1,0:T(8,128)(2,1)S(1)}, u32[]{:S(2)}, u32[]{:S(2)}) collective-permute-start(bf16[112,768]{1,0:T(8,128)(2,1)S(1)} %get-tuple-element.114), channel_id=1, source_target_pairs={{0,16},{8,24},{16,0},{24,8},{32,48},{40,56},{48,32},{56,40},{64,80... | collective-permute-start | bytes 516104 | tf_op jit(solution)/shard_map/ppermute | solution.py:29
  120.4 22.2 %collective-permute-start.34 = (bf16[304,768]{1,0:T(8,128)(2,1)S(1)}, bf16[304,768]{1,0:T(8,128)(2,1)S(1)}, u32[]{:S(2)}, u32[]{:S(2)}) collective-permute-start(bf16[304,768]{1,0:T(8,128)(2,1)S(1)} %get-tuple-element.120), channel_id=1, source_target_pairs={{0,32},{8,40},{16,48},{24,56},{32,64},{40,72},{48,80},{56,88},{64,... | collective-permute-start | bytes 1400840 | tf_op jit(solution)/shard_map/ppermute | solution.py:35
  123.0 19.5 %collective-permute-start.35 = (bf16[304,768]{1,0:T(8,128)(2,1)S(1)}, bf16[304,768]{1,0:T(8,128)(2,1)S(1)}, u32[]{:S(2)}, u32[]{:S(2)}) collective-permute-start(bf16[304,768]{1,0:T(8,128)(2,1)S(1)} %get-tuple-element.121), channel_id=1, source_target_pairs={{32,0},{40,8},{48,16},{56,24},{64,32},{72,40},{80,48},{88,56},{96,... | collective-permute-start | bytes 1400840 | tf_op jit(solution)/shard_map/ppermute | solution.py:35
  133.4 12.4 %collective-permute-start.30 = (f32[8,128]{1,0:T(8,128)S(1)}, f32[8,128]{1,0:T(8,128)S(1)}, u32[]{:S(2)}, u32[]{:S(2)}) collective-permute-start(f32[8,128]{1,0:T(8,128)S(1)} %add_add_fusion.3), channel_id=1, source_target_pairs={{0,96},{8,104},{16,112},{24,120},{32,0},{40,8},{48,16},{56,24},{64... | collective-permute-start | bytes 12296 | tf_op jit(solution)/shard_map/ppermute | solution.py:40
  144.5 10.2 %collective-permute-start.44 = (bf16[288,768]{1,0:T(8,128)(2,1)S(1)}, bf16[288,768]{1,0:T(8,128)(2,1)S(1)}, u32[]{:S(2)}, u32[]{:S(2)}) collective-permute-start(bf16[288,768]{1,0:T(8,128)(2,1)S(1)} %get-tuple-element.145), channel_id=1, source_target_pairs={{32,0},{40,8},{48,16},{56,24},{64,32},{72,40},{80,48},{88,56},{96,... | collective-permute-start | bytes 1327112 | tf_op jit(solution)/shard_map/ppermute | solution.py:35
  147.5 10.3 %collective-permute-start.38 = (f16[96,768]{1,0:T(8,128)(2,1)S(1)}, f16[96,768]{1,0:T(8,128)(2,1)S(1)}, u32[]{:S(2)}, u32[]{:S(2)}) collective-permute-start(f16[96,768]{1,0:T(8,128)(2,1)S(1)} %get-tuple-element.160), channel_id=1, source_target_pairs={{0,24},{8,0},{16,8},{24,16},{32,56},{40,32},{48,40},{56,48},{64,88... | collective-permute-start | bytes 442376 | tf_op jit(solution)/shard_map/ppermute | solution.py:29
  148.0 10.7 %collective-permute-start.37 = (f16[96,768]{1,0:T(8,128)(2,1)S(1)}, f16[96,768]{1,0:T(8,128)(2,1)S(1)}, u32[]{:S(2)}, u32[]{:S(2)}) collective-permute-start(f16[96,768]{1,0:T(8,128)(2,1)S(1)} %get-tuple-element.161), channel_id=1, source_target_pairs={{0,16},{8,24},{16,0},{24,8},{32,48},{40,56},{48,32},{56,40},{64,80... | collective-permute-start | bytes 442376 | tf_op jit(solution)/shard_map/ppermute | solution.py:29
  149.2 9.5 %collective-permute-start.36 = (f16[96,768]{1,0:T(8,128)(2,1)S(1)}, f16[96,768]{1,0:T(8,128)(2,1)S(1)}, u32[]{:S(2)}, u32[]{:S(2)}) collective-permute-start(f16[96,768]{1,0:T(8,128)(2,1)S(1)} %get-tuple-element.162), channel_id=1, source_target_pairs={{0,8},{8,16},{16,24},{24,0},{32,40},{40,48},{48,56},{56,32},{64,72... | collective-permute-start | bytes 442376 | tf_op jit(solution)/shard_map/ppermute | solution.py:29
  156.4 9.9 %collective-permute-start.47 = (f16[96,768]{1,0:T(8,128)(2,1)S(1)}, f16[96,768]{1,0:T(8,128)(2,1)S(1)}, u32[]{:S(2)}, u32[]{:S(2)}) collective-permute-start(f16[96,768]{1,0:T(8,128)(2,1)S(1)} %get-tuple-element.156), channel_id=1, source_target_pairs={{0,24},{8,0},{16,8},{24,16},{32,56},{40,32},{48,40},{56,48},{64,88... | collective-permute-start | bytes 442376 | tf_op jit(solution)/shard_map/ppermute | solution.py:29
  156.5 9.8 %collective-permute-start.46 = (f16[96,768]{1,0:T(8,128)(2,1)S(1)}, f16[96,768]{1,0:T(8,128)(2,1)S(1)}, u32[]{:S(2)}, u32[]{:S(2)}) collective-permute-start(f16[96,768]{1,0:T(8,128)(2,1)S(1)} %get-tuple-element.157), channel_id=1, source_target_pairs={{0,16},{8,24},{16,0},{24,8},{32,48},{40,56},{48,32},{56,40},{64,80... | collective-permute-start | bytes 442376 | tf_op jit(solution)/shard_map/ppermute | solution.py:29
  161.1 11.1 %collective-permute-start.39 = (f16[4,48,768]{2,1,0:T(8,128)(2,1)S(1)}, f16[4,48,768]{2,1,0:T(8,128)(2,1)S(1)}, u32[]{:S(2)}, u32[]{:S(2)}) collective-permute-start(f16[4,48,768]{2,1,0:T(8,128)(2,1)S(1)} %convert_element_type.115), channel_id=1, source_target_pairs={{0,1},{1,0},{2,3},{3,2},{4,5},{5,4},{6,7},{7,6},{8,9},{9,8},{10,11... | collective-permute-start | bytes 884744 | tf_op jit(solution)/shard_map/ppermute | solution.py:53
  188.0 9.7 %collective-permute-start.52 = (f16[2,48,768]{2,1,0:T(8,128)(2,1)S(1)}, f16[2,48,768]{2,1,0:T(8,128)(2,1)S(1)}, u32[]{:S(2)}, u32[]{:S(2)}) collective-permute-start(f16[2,48,768]{2,1,0:T(8,128)(2,1)S(1)} %fusion.10), channel_id=1, source_target_pairs={{0,2},{1,3},{2,4},{3,5},{4,6},{5,7},{6,0},{7,1},{8,10},{9,11},{10,... | collective-permute-start | bytes 442376 | tf_op jit(solution)/shard_map/ppermute | solution.py:49
  (53 other events, 290.1 us)
where the time goes:
time: 219 us; the launch traced here: 216 us
  starting transfers between devices  97.1 us (44%)
  waiting for transfers between devices  51.9 us (24%)
  Pallas kernels  33.1 us (15%)
  local copies, waits for them, and re-layouts  13.1 us (6%)
  other arithmetic  12.7 us (6%)
  between operations  8.27 us (4%)
    pallas_call x19, Pallas kernels, call(): pl.pallas_call(body, out_shape=shapes, in_specs=[in_smem] * len(smem) + [...  33.1 us
    ppermute x30, starting transfers between devices, along_x(): return lax.ppermute(block, 'sector', route)  31.2 us
    ppermute x6, starting transfers between devices, other_core(): return lax.ppermute(block, 'mpo', [(i, i ^ 1) for i in range(2 * SIDE)])  21.8 us
    ppermute x12, waiting for transfers between devices, along_y(): return lax.ppermute(block, 'mpo', route)  19.4 us
    ppermute x8, starting transfers between devices, along_z(): return lax.ppermute(block, 'sector', route)  18.5 us
    ppermute x30, waiting for transfers between devices, along_x(): return lax.ppermute(block, 'sector', route)  16.7 us
    ppermute x12, starting transfers between devices, along_y(): return lax.ppermute(block, 'mpo', route)  13.7 us
    ppermute x6, starting transfers between devices, around_z(): lax.ppermute(block, 'sector', [(i, (i + SIDE * step) % count) for i in ra...  11.9 us
  transfers between devices with their start and end apart: 62, of which 28 were waited for; matrix products, arithmetic and copies ran while one was open for 5% of the time, Pallas kernels for 11%

commit v1 on v0

--- a/solution.py
+++ b/solution.py
@@ -85,17 +85,26 @@
     return jnp.dot(a, b, preferred_element_type=F32)
 
 
-def product_kernel(row, noted, place, left, vector, squares, *refs):
+def product_kernel(row, noted, given, place, left, vector, *refs):
+    if given:
+        squares, *refs = refs
     outs, acc = refs[:SIDE], refs[-1]
     rows, m = acc.shape
     part = rows // SIDE
     left_head, left_tail = halves_of(left[pl.ds(row, rows), :])
     wide = m // 3
+    total = jnp.zeros((8, wide), F32)
     for n in range(3):
         cols = slice(n * wide, (n + 1) * wide)
-        head, tail = halves_of(vector[:, cols])
+        value = vector[:, cols]
+        if not given:
+            total = total + jnp.sum((value * value).reshape(-1, 8, wide), axis=0)
+        head, tail = halves_of(value)
         acc[:, cols] = dot(left_head, head) + (dot(left_head, tail) + dot(left_tail, head))
     x = place[0]
+    if not given:
+        squares = refs[SIDE]
+        squares[...] = jnp.full(squares.shape, jnp.sum(total), F32)
     if noted:
         power = jnp.ceil(0.5 * jnp.log2(jnp.clip(squares[...], 1e-36, 1e36)) + 0.01)
         note = jnp.broadcast_to(power[:1, :1] + NOTE, (TILE, m)).astype(BF16)
@@ -104,18 +113,6 @@
         outs[d][:part, :] = acc[pl.ds(start, part), :].astype(BF16)
         if noted:
             outs[d][part:, :] = note
-
-
-def squares_kernel(vector, out):
-    rows, m = vector.shape
-    step_rows = 64
-
-    def step(i, total):
-        value = vector[pl.ds(pl.multiple_of(i * step_rows, step_rows), step_rows), :]
-        return total + jnp.sum((value * value).reshape(-1, 8, m), axis=0)
-
-    total = lax.fori_loop(0, rows // step_rows, step, jnp.zeros((8, m), F32))
-    out[...] = jnp.full(out.shape, jnp.sum(total), F32)
 
 
 def select_kernel(part, skips, *refs):
@@ -316,17 +313,21 @@
 
     def products(chunk, vector, squares):
         noted = chunk == 0
+        given = squares is not None
         return call(
-            functools.partial(product_kernel, chunk * rows, noted),
-            [((part + TILE * noted, m), BF16)] * SIDE,
+            functools.partial(product_kernel, chunk * rows, noted, given),
+            [((part + TILE * noted, m), BF16)] * SIDE + [((8, 128), F32)] * (not given),
             [place],
-            [left, vector, squares],
+            [left, vector] + [squares] * given,
             [pltpu.VMEM((rows, m), F32)],
             flops,
         )
 
     def hamiltonian(vector, squares, summed):
-        pieces = [products(c, vector, squares) for c in range(CHUNKS)]
+        pieces = [list(products(0, vector, squares))]
+        if squares is None:
+            squares = pieces[0].pop()
+        pieces += [products(c, vector, squares) for c in range(1, CHUNKS)]
         near, beyond, mixed, note, total = [], [], [], None, squares
         for p in pieces:
             near.append(after(spread(after(p, near[-1:])), pieces[-1][0]))
@@ -353,9 +354,8 @@
     h_scale = F16_TOP / (8.4 * reach * reach * spread_of)
     small = F32(1e-18)
 
-    squares = call(squares_kernel, [((8, 128), F32)], [], [psi])[0]
+    piece, power, squares = hamiltonian(psi, None, False)
     psi_norm = jnp.sqrt(squares[0, 0]) + small
-    piece, power, _ = hamiltonian(psi, squares, False)
     bound = F16_TOP / (1.05 * (power * (F16_TOP / h_scale) + 2.0 * psi_norm))
     piece = piece * (power * (bound / h_scale)) - (bound * recurrence[0]) * own_rows(psi)
     resid, squares = share_bonds(piece.astype(F16), 1.0 / bound)

time: 219 us -> 214 us (0.977)
  Pallas kernels: 33.1 us -> 30 us
    pallas_call x19 -> x18, Pallas kernels: 33.1 us -> 30 us  [call(): pl.pallas_call(body, out_shape=shapes, in_specs=[in_smem] * len(smem) + [...]
    unnamed x32 -> x26, local copies, waits for them, and re-layouts: 6.96 us -> 5.76 us
  transfers between devices with their start and end apart: 62 -> 62, of which waited for: 28 -> 29; matrix products, arithmetic and copies ran while one was open for 5% -> 5% of each run, Pallas kernels for 11% -> 10%
where the time goes in v1:
time: 214 us; the launch traced here: 211 us
  starting transfers between devices  96.1 us (45%)
  waiting for transfers between devices  52.9 us (25%)
  Pallas kernels  30 us (14%)
  other arithmetic  12.7 us (6%)
  local copies, waits for them, and re-layouts  11 us (5%)
  between operations  8.13 us (4%)
    ppermute x30, starting transfers between devices, along_x(): return lax.ppermute(block, 'sector', route)  32.3 us
    pallas_call x18, Pallas kernels, call(): pl.pallas_call(body, out_shape=shapes, in_specs=[in_smem] * len(smem) + [...  30 us
    ppermute x6, starting transfers between devices, other_core(): return lax.ppermute(block, 'mpo', [(i, i ^ 1) for i in range(2 * SIDE)])  22.2 us
    ppermute x12, waiting for transfers between devices, along_y(): return lax.ppermute(block, 'mpo', route)  19.3 us
    ppermute x30, waiting for transfers between devices, along_x(): return lax.ppermute(block, 'sector', route)  17.7 us
    ppermute x8, starting transfers between devices, along_z(): return lax.ppermute(block, 'sector', route)  17.6 us
    ppermute x12, starting transfers between devices, along_y(): return lax.ppermute(block, 'mpo', route)  13.8 us
    ppermute x6, starting transfers between devices, around_z(): lax.ppermute(block, 'sector', [(i, (i + SIDE * step) % count) for i in ra...  10.2 us
  transfers between devices with their start and end apart: 62, of which 29 were waited for; matrix products, arithmetic and copies ran while one was open for 5% of the time, Pallas kernels for 10%

profile of v1, /device:TPU:1, one launch (start us, length us, event | category | flops | bytes accessed | tf_op | source)
XLA Modules:
  0.0 210.8 jit_solution(13968476958710109751)
XLA Ops:
  4.1 3.0 %shard_map.95 = (bf16[112,768]{1,0:T(8,128)(2,1)S(1)}, bf16[112,768]{1,0:T(8,128)(2,1)}, bf16[112,768]{1,0:T(8,128)(2,1)S(1)}, bf16[112,768]{1,0:T(8,128)(2,1)S(1)}, f32[8,128]{1,0:T(8,128)S(1)}) custom-call(s32[3]{0:T(128)S(1)} %get-tuple-element.193.place, f32[768,768]{1,0:T(8,128)S(1)} %bitcast.127, f32[768,768]{1,0:T(8,128)S(1)} %bitcast.125), custom_call_target="tpu_custom_call" | custom-call | flops 1358954496 | bytes 5410816 | tf_op jit(solution)/shard_map/pallas_call | solution.py:68
  9.1 2.5 %collective-permute-start.1 = (bf16[112,768]{1,0:T(8,128)(2,1)S(1)}, bf16[112,768]{1,0:T(8,128)(2,1)S(1)}, u32[]{:S(2)}, u32[]{:S(2)}) collective-permute-start(bf16[112,768]{1,0:T(8,128)(2,1)S(1)} %get-tuple-element.87), channel_id=1, source_target_pairs={{0,16},{8,24},{16,0},{24,8},{32,48},{40,56},{48,32},{56,40},{64,80... | collective-permute-start | bytes 516104 | tf_op jit(solution)/shard_map/ppermute | solution.py:29
  16.9 2.3 %collective-permute-done.1.refs_2_ = bf16[112,768]{1,0:T(8,128)(2,1)S(1)} collective-permute-done((bf16[112,768]{1,0:T(8,128)(2,1)S(1)}, bf16[112,768]{1,0:T(8,128)(2,1)S(1)}, u32[]{:S(2)}, u32[]{:S(2)}) %collective-permute-start.1) | collective-permute-done | bytes 172064 | tf_op jit(solution)/shard_map/ppermute | solution.py:29
  19.9 3.5 %collective-permute-start.3 = (bf16[304,768]{1,0:T(8,128)(2,1)S(1)}, bf16[304,768]{1,0:T(8,128)(2,1)S(1)}, u32[]{:S(2)}, u32[]{:S(2)}) collective-permute-start(bf16[304,768]{1,0:T(8,128)(2,1)S(1)} %get-tuple-element.95), channel_id=1, source_target_pairs={{0,32},{8,40},{16,48},{24,56},{32,64},{40,72},{48,80},{56,88},{64,... | collective-permute-start | bytes 1400840 | tf_op jit(solution)/shard_map/ppermute | solution.py:35
  36.3 4.1 %collective-permute-start.12 = (bf16[288,768]{1,0:T(8,128)(2,1)}, bf16[288,768]{1,0:T(8,128)(2,1)S(1)}, u32[]{:S(2)}, u32[]{:S(2)}) collective-permute-start(bf16[288,768]{1,0:T(8,128)(2,1)} %get-tuple-element.114), channel_id=1, source_target_pairs={{0,32},{8,40},{16,48},{24,56},{32,64},{40,72},{48,80},{56,88},{64,... | collective-permute-start | bytes 1327112 | tf_op jit(solution)/shard_map/ppermute | solution.py:35
  47.3 3.8 %collective-permute-done.13.refs_5_ = bf16[288,768]{1,0:T(8,128)(2,1)S(1)} collective-permute-done((bf16[288,768]{1,0:T(8,128)(2,1)}, bf16[288,768]{1,0:T(8,128)(2,1)S(1)}, u32[]{:S(2)}, u32[]{:S(2)}) %collective-permute-start.13) | collective-permute-done | bytes 442400 | tf_op jit(solution)/shard_map/ppermute | solution.py:35
  58.7 4.6 %collective-permute-start.8 = (f16[4,48,768]{2,1,0:T(8,128)(2,1)S(1)}, f16[4,48,768]{2,1,0:T(8,128)(2,1)S(1)}, u32[]{:S(2)}, u32[]{:S(2)}) collective-permute-start(f16[4,48,768]{2,1,0:T(8,128)(2,1)S(1)} %convert_element_type.100), channel_id=1, source_target_pairs={{0,1},{1,0},{2,3},{3,2},{4,5},{5,4},{6,7},{7,6},{8,9},{9,8},{10,11... | collective-permute-start | bytes 884744 | tf_op jit(solution)/shard_map/ppermute | solution.py:53
  65.7 3.9 %collective-permute-start.17 = (f16[4,48,768]{2,1,0:T(8,128)(2,1)S(1)}, f16[4,48,768]{2,1,0:T(8,128)(2,1)S(1)}, u32[]{:S(2)}, u32[]{:S(2)}) collective-permute-start(f16[4,48,768]{2,1,0:T(8,128)(2,1)S(1)} %convert_element_type.104), channel_id=1, source_target_pairs={{0,1},{1,0},{2,3},{3,2},{4,5},{5,4},{6,7},{7,6},{8,9},{9,8},{10,11... | collective-permute-start | bytes 884744 | tf_op jit(solution)/shard_map/ppermute | solution.py:53
  79.4 2.4 %collective-permute-done.19 = f16[2,48,768]{2,1,0:T(8,128)(2,1)S(1)} collective-permute-done((f16[2,48,768]{2,1,0:T(8,128)(2,1)S(1)}, f16[2,48,768]{2,1,0:T(8,128)(2,1)S(1)}, u32[]{:S(2)}, u32[]{:S(2)}) %collective-permute-start.19) | collective-permute-done | bytes 147488 | tf_op jit(solution)/shard_map/ppermute | solution.py:49
  87.0 2.5 %collective-permute-done.22 = f16[2,48,768]{2,1,0:T(8,128)(2,1)S(1)} collective-permute-done((f16[2,48,768]{2,1,0:T(8,128)(2,1)S(1)}, f16[2,48,768]{2,1,0:T(8,128)(2,1)S(1)}, u32[]{:S(2)}, u32[]{:S(2)}) %collective-permute-start.22) | collective-permute-done | bytes 147488 | tf_op jit(solution)/shard_map/ppermute | solution.py:49
  89.4 2.3 %collective-permute-done.21 = f16[2,48,768]{2,1,0:T(8,128)(2,1)S(1)} collective-permute-done((f16[2,48,768]{2,1,0:T(8,128)(2,1)S(1)}, f16[2,48,768]{2,1,0:T(8,128)(2,1)S(1)}, u32[]{:S(2)}, u32[]{:S(2)}) %collective-permute-start.21) | collective-permute-done | bytes 147488 | tf_op jit(solution)/shard_map/ppermute | solution.py:49
  92.0 3.2 %collective-permute-start.24 = (f16[4,2,48,768]{3,2,1,0:T(8,128)(2,1)S(1)}, f16[4,2,48,768]{3,2,1,0:T(8,128)(2,1)S(1)}, u32[]{:S(2)}, u32[]{:S(2)}) collective-permute-start(f16[4,2,48,768]{3,2,1,0:T(8,128)(2,1)S(1)} %get-tuple-element.173), channel_id=1, source_target_pairs={{0,1},{1,0},{2,3},{3,2},{4,5},{5,4},{6,7},{7,6},{8,9},{9,8},{10,11... | collective-permute-start | bytes 1769480 | tf_op jit(solution)/shard_map/ppermute | solution.py:53
  105.8 5.5 %collective-permute-done.31.refs_1_ = bf16[112,768]{1,0:T(8,128)(2,1)S(1)} collective-permute-done((bf16[112,768]{1,0:T(8,128)(2,1)S(1)}, bf16[112,768]{1,0:T(8,128)(2,1)S(1)}, u32[]{:S(2)}, u32[]{:S(2)}) %collective-permute-start.31) | collective-permute-done | bytes 172064 | tf_op jit(solution)/shard_map/ppermute | solution.py:29
  112.3 3.2 %collective-permute-start.34 = (bf16[304,768]{1,0:T(8,128)(2,1)S(1)}, bf16[304,768]{1,0:T(8,128)(2,1)S(1)}, u32[]{:S(2)}, u32[]{:S(2)}) collective-permute-start(bf16[304,768]{1,0:T(8,128)(2,1)S(1)} %get-tuple-element.130), channel_id=1, source_target_pairs={{0,32},{8,40},{16,48},{24,56},{32,64},{40,72},{48,80},{56,88},{64,... | collective-permute-start | bytes 1400840 | tf_op jit(solution)/shard_map/ppermute | solution.py:35
  116.8 2.8 %collective-permute-start.27 = (f32[8,128]{1,0:T(8,128)S(1)}, f32[8,128]{1,0:T(8,128)S(1)}, u32[]{:S(2)}, u32[]{:S(2)}) collective-permute-start(f32[8,128]{1,0:T(8,128)S(1)} %get-tuple-element.121.refs_0_), channel_id=1, source_target_pairs={{0,24},{8,0},{16,8},{24,16},{32,56},{40,32},{48,40},{56,48},{64,88... | collective-permute-start | bytes 12296 | tf_op jit(solution)/shard_map/ppermute | solution.py:29
  125.9 2.6 %collective-permute-start.30 = (f32[8,128]{1,0:T(8,128)S(1)}, f32[8,128]{1,0:T(8,128)S(1)}, u32[]{:S(2)}, u32[]{:S(2)}) collective-permute-start(f32[8,128]{1,0:T(8,128)S(1)} %add_add_fusion.3), channel_id=1, source_target_pairs={{0,96},{8,104},{16,112},{24,120},{32,0},{40,8},{48,16},{56,24},{64... | collective-permute-start | bytes 12296 | tf_op jit(solution)/shard_map/ppermute | solution.py:40
  130.1 3.4 %collective-permute-start.29 = (f32[8,128]{1,0:T(8,128)S(1)}, f32[8,128]{1,0:T(8,128)S(1)}, u32[]{:S(2)}, u32[]{:S(2)}) collective-permute-start(f32[8,128]{1,0:T(8,128)S(1)} %add_add_fusion.3), channel_id=1, source_target_pairs={{0,64},{8,72},{16,80},{24,88},{32,96},{40,104},{48,112},{56,120},{... | collective-permute-start | bytes 12296 | tf_op jit(solution)/shard_map/ppermute | solution.py:40
  142.0 4.0 %collective-permute-done.44.refs_5_ = bf16[288,768]{1,0:T(8,128)(2,1)S(1)} collective-permute-done((bf16[288,768]{1,0:T(8,128)(2,1)S(1)}, bf16[288,768]{1,0:T(8,128)(2,1)S(1)}, u32[]{:S(2)}, u32[]{:S(2)}) %collective-permute-start.44) | collective-permute-done | bytes 442400 | tf_op jit(solution)/shard_map/ppermute | solution.py:35
  152.5 5.6 %collective-permute-start.39 = (f16[4,48,768]{2,1,0:T(8,128)(2,1)S(1)}, f16[4,48,768]{2,1,0:T(8,128)(2,1)S(1)}, u32[]{:S(2)}, u32[]{:S(2)}) collective-permute-start(f16[4,48,768]{2,1,0:T(8,128)(2,1)S(1)} %convert_element_type.115), channel_id=1, source_target_pairs={{0,1},{1,0},{2,3},{3,2},{4,5},{5,4},{6,7},{7,6},{8,9},{9,8},{10,11... | collective-permute-start | bytes 884744 | tf_op jit(solution)/shard_map/ppermute | solution.py:53
  160.5 4.0 %collective-permute-start.48 = (f16[4,48,768]{2,1,0:T(8,128)(2,1)S(1)}, f16[4,48,768]{2,1,0:T(8,128)(2,1)S(1)}, u32[]{:S(2)}, u32[]{:S(2)}) collective-permute-start(f16[4,48,768]{2,1,0:T(8,128)(2,1)S(1)} %convert_element_type.119), channel_id=1, source_target_pairs={{0,1},{1,0},{2,3},{3,2},{4,5},{5,4},{6,7},{7,6},{8,9},{9,8},{10,11... | collective-permute-start | bytes 884744 | tf_op jit(solution)/shard_map/ppermute | solution.py:53
  166.6 2.7 %collective-permute-start.51 = (f16[2,48,768]{2,1,0:T(8,128)(2,1)}, f16[2,48,768]{2,1,0:T(8,128)(2,1)}, u32[]{:S(2)}, u32[]{:S(2)}) collective-permute-start(f16[2,48,768]{2,1,0:T(8,128)(2,1)} %get-tuple-element.163), channel_id=1, source_target_pairs={{0,6},{1,7},{2,0},{3,1},{4,2},{5,3},{6,4},{7,5},{8,14},{9,15},{10,... | collective-permute-start | bytes 442376 | tf_op jit(solution)/shard_map/ppermute | solution.py:49
  176.9 3.4 %collective-permute-start.54 = (f16[2,48,768]{2,1,0:T(8,128)(2,1)S(1)}, f16[2,48,768]{2,1,0:T(8,128)(2,1)S(1)}, u32[]{:S(2)}, u32[]{:S(2)}) collective-permute-start(f16[2,48,768]{2,1,0:T(8,128)(2,1)S(1)} %fusion.10), channel_id=1, source_target_pairs={{0,6},{1,7},{2,0},{3,1},{4,2},{5,3},{6,4},{7,5},{8,14},{9,15},{10,... | collective-permute-start | bytes 442376 | tf_op jit(solution)/shard_map/ppermute | solution.py:49
  181.0 3.0 %collective-permute-done.54 = f16[2,48,768]{2,1,0:T(8,128)(2,1)S(1)} collective-permute-done((f16[2,48,768]{2,1,0:T(8,128)(2,1)S(1)}, f16[2,48,768]{2,1,0:T(8,128)(2,1)S(1)}, u32[]{:S(2)}, u32[]{:S(2)}) %collective-permute-start.54) | collective-permute-done | bytes 147488 | tf_op jit(solution)/shard_map/ppermute | solution.py:49
  186.0 4.1 %collective-permute-done.52 = f16[2,48,768]{2,1,0:T(8,128)(2,1)S(1)} collective-permute-done((f16[2,48,768]{2,1,0:T(8,128)(2,1)S(1)}, f16[2,48,768]{2,1,0:T(8,128)(2,1)S(1)}, u32[]{:S(2)}, u32[]{:S(2)}) %collective-permute-start.52) | collective-permute-done | bytes 147488 | tf_op jit(solution)/shard_map/ppermute | solution.py:49
  (201 shorter events, 120.2 us)
Async XLA Ops:
  7.1 9.8 %collective-permute-start = (bf16[112,768]{1,0:T(8,128)(2,1)}, bf16[112,768]{1,0:T(8,128)(2,1)S(1)}, u32[]{:S(2)}, u32[]{:S(2)}) collective-permute-start(bf16[112,768]{1,0:T(8,128)(2,1)} %get-tuple-element.86), channel_id=1, source_target_pairs={{0,8},{8,16},{16,24},{24,0},{32,40},{40,48},{48,56},{56,32},{64,72... | collective-permute-start | bytes 516104 | tf_op jit(solution)/shard_map/ppermute | solution.py:29
  9.1 10.1 %collective-permute-start.1 = (bf16[112,768]{1,0:T(8,128)(2,1)S(1)}, bf16[112,768]{1,0:T(8,128)(2,1)S(1)}, u32[]{:S(2)}, u32[]{:S(2)}) collective-permute-start(bf16[112,768]{1,0:T(8,128)(2,1)S(1)} %get-tuple-element.87), channel_id=1, source_target_pairs={{0,16},{8,24},{16,0},{24,8},{32,48},{40,56},{48,32},{56,40},{64,80... | collective-permute-start | bytes 516104 | tf_op jit(solution)/shard_map/ppermute | solution.py:29
  19.9 16.3 %collective-permute-start.3 = (bf16[304,768]{1,0:T(8,128)(2,1)S(1)}, bf16[304,768]{1,0:T(8,128)(2,1)S(1)}, u32[]{:S(2)}, u32[]{:S(2)}) collective-permute-start(bf16[304,768]{1,0:T(8,128)(2,1)S(1)} %get-tuple-element.95), channel_id=1, source_target_pairs={{0,32},{8,40},{16,48},{24,56},{32,64},{40,72},{48,80},{56,88},{64,... | collective-permute-start | bytes 1400840 | tf_op jit(solution)/shard_map/ppermute | solution.py:35
  23.5 12.8 %collective-permute-start.4 = (bf16[304,768]{1,0:T(8,128)(2,1)S(1)}, bf16[304,768]{1,0:T(8,128)(2,1)S(1)}, u32[]{:S(2)}, u32[]{:S(2)}) collective-permute-start(bf16[304,768]{1,0:T(8,128)(2,1)S(1)} %get-tuple-element.96), channel_id=1, source_target_pairs={{32,0},{40,8},{48,16},{56,24},{64,32},{72,40},{80,48},{88,56},{96,... | collective-permute-start | bytes 1400840 | tf_op jit(solution)/shard_map/ppermute | solution.py:35
  36.3 11.1 %collective-permute-start.12 = (bf16[288,768]{1,0:T(8,128)(2,1)}, bf16[288,768]{1,0:T(8,128)(2,1)S(1)}, u32[]{:S(2)}, u32[]{:S(2)}) collective-permute-start(bf16[288,768]{1,0:T(8,128)(2,1)} %get-tuple-element.114), channel_id=1, source_target_pairs={{0,32},{8,40},{16,48},{24,56},{32,64},{40,72},{48,80},{56,88},{64,... | collective-permute-start | bytes 1327112 | tf_op jit(solution)/shard_map/ppermute | solution.py:35
  40.3 10.8 %collective-permute-start.13 = (bf16[288,768]{1,0:T(8,128)(2,1)}, bf16[288,768]{1,0:T(8,128)(2,1)S(1)}, u32[]{:S(2)}, u32[]{:S(2)}) collective-permute-start(bf16[288,768]{1,0:T(8,128)(2,1)} %get-tuple-element.115), channel_id=1, source_target_pairs={{32,0},{40,8},{48,16},{56,24},{64,32},{72,40},{80,48},{88,56},{96,... | collective-permute-start | bytes 1327112 | tf_op jit(solution)/shard_map/ppermute | solution.py:35
  43.8 11.7 %collective-permute-start.7 = (f16[96,768]{1,0:T(8,128)(2,1)S(1)}, f16[96,768]{1,0:T(8,128)(2,1)S(1)}, u32[]{:S(2)}, u32[]{:S(2)}) collective-permute-start(f16[96,768]{1,0:T(8,128)(2,1)S(1)} %get-tuple-element.183), channel_id=1, source_target_pairs={{0,24},{8,0},{16,8},{24,16},{32,56},{40,32},{48,40},{56,48},{64,88... | collective-permute-start | bytes 442376 | tf_op jit(solution)/shard_map/ppermute | solution.py:29
  45.8 10.5 %collective-permute-start.6 = (f16[96,768]{1,0:T(8,128)(2,1)S(1)}, f16[96,768]{1,0:T(8,128)(2,1)S(1)}, u32[]{:S(2)}, u32[]{:S(2)}) collective-permute-start(f16[96,768]{1,0:T(8,128)(2,1)S(1)} %get-tuple-element.184), channel_id=1, source_target_pairs={{0,16},{8,24},{16,0},{24,8},{32,48},{40,56},{48,32},{56,40},{64,80... | collective-permute-start | bytes 442376 | tf_op jit(solution)/shard_map/ppermute | solution.py:29
  46.1 10.2 %collective-permute-start.5 = (f16[96,768]{1,0:T(8,128)(2,1)S(1)}, f16[96,768]{1,0:T(8,128)(2,1)S(1)}, u32[]{:S(2)}, u32[]{:S(2)}) collective-permute-start(f16[96,768]{1,0:T(8,128)(2,1)S(1)} %get-tuple-element.185), channel_id=1, source_target_pairs={{0,8},{8,16},{16,24},{24,0},{32,40},{40,48},{48,56},{56,32},{64,72... | collective-permute-start | bytes 442376 | tf_op jit(solution)/shard_map/ppermute | solution.py:29
  52.8 10.5 %collective-permute-start.16 = (f16[96,768]{1,0:T(8,128)(2,1)S(1)}, f16[96,768]{1,0:T(8,128)(2,1)S(1)}, u32[]{:S(2)}, u32[]{:S(2)}) collective-permute-start(f16[96,768]{1,0:T(8,128)(2,1)S(1)} %get-tuple-element.179), channel_id=1, source_target_pairs={{0,24},{8,0},{16,8},{24,16},{32,56},{40,32},{48,40},{56,48},{64,88... | collective-permute-start | bytes 442376 | tf_op jit(solution)/shard_map/ppermute | solution.py:29
  58.7 11.0 %collective-permute-start.8 = (f16[4,48,768]{2,1,0:T(8,128)(2,1)S(1)}, f16[4,48,768]{2,1,0:T(8,128)(2,1)S(1)}, u32[]{:S(2)}, u32[]{:S(2)}) collective-permute-start(f16[4,48,768]{2,1,0:T(8,128)(2,1)S(1)} %convert_element_type.100), channel_id=1, source_target_pairs={{0,1},{1,0},{2,3},{3,2},{4,5},{5,4},{6,7},{7,6},{8,9},{9,8},{10,11... | collective-permute-start | bytes 884744 | tf_op jit(solution)/shard_map/ppermute | solution.py:53
  100.8 10.6 %collective-permute-start.31 = (bf16[112,768]{1,0:T(8,128)(2,1)S(1)}, bf16[112,768]{1,0:T(8,128)(2,1)S(1)}, u32[]{:S(2)}, u32[]{:S(2)}) collective-permute-start(bf16[112,768]{1,0:T(8,128)(2,1)S(1)} %get-tuple-element.123), channel_id=1, source_target_pairs={{0,8},{8,16},{16,24},{24,0},{32,40},{40,48},{48,56},{56,32},{64,72... | collective-permute-start | bytes 516104 | tf_op jit(solution)/shard_map/ppermute | solution.py:29
  100.9 10.5 %collective-permute-start.32 = (bf16[112,768]{1,0:T(8,128)(2,1)S(1)}, bf16[112,768]{1,0:T(8,128)(2,1)S(1)}, u32[]{:S(2)}, u32[]{:S(2)}) collective-permute-start(bf16[112,768]{1,0:T(8,128)(2,1)S(1)} %get-tuple-element.124), channel_id=1, source_target_pairs={{0,16},{8,24},{16,0},{24,8},{32,48},{40,56},{48,32},{56,40},{64,80... | collective-permute-start | bytes 516104 | tf_op jit(solution)/shard_map/ppermute | solution.py:29
  102.3 9.4 %collective-permute-start.33 = (bf16[112,768]{1,0:T(8,128)(2,1)S(1)}, bf16[112,768]{1,0:T(8,128)(2,1)S(1)}, u32[]{:S(2)}, u32[]{:S(2)}) collective-permute-start(bf16[112,768]{1,0:T(8,128)(2,1)S(1)} %get-tuple-element.125), channel_id=1, source_target_pairs={{0,24},{8,0},{16,8},{24,16},{32,56},{40,32},{48,40},{56,48},{64,88... | collective-permute-start | bytes 516104 | tf_op jit(solution)/shard_map/ppermute | solution.py:29
  112.3 21.9 %collective-permute-start.34 = (bf16[304,768]{1,0:T(8,128)(2,1)S(1)}, bf16[304,768]{1,0:T(8,128)(2,1)S(1)}, u32[]{:S(2)}, u32[]{:S(2)}) collective-permute-start(bf16[304,768]{1,0:T(8,128)(2,1)S(1)} %get-tuple-element.130), channel_id=1, source_target_pairs={{0,32},{8,40},{16,48},{24,56},{32,64},{40,72},{48,80},{56,88},{64,... | collective-permute-start | bytes 1400840 | tf_op jit(solution)/shard_map/ppermute | solution.py:35
  115.5 18.7 %collective-permute-start.35 = (bf16[304,768]{1,0:T(8,128)(2,1)S(1)}, bf16[304,768]{1,0:T(8,128)(2,1)S(1)}, u32[]{:S(2)}, u32[]{:S(2)}) collective-permute-start(bf16[304,768]{1,0:T(8,128)(2,1)S(1)} %get-tuple-element.131), channel_id=1, source_target_pairs={{32,0},{40,8},{48,16},{56,24},{64,32},{72,40},{80,48},{88,56},{96,... | collective-permute-start | bytes 1400840 | tf_op jit(solution)/shard_map/ppermute | solution.py:35
  125.9 11.3 %collective-permute-start.30 = (f32[8,128]{1,0:T(8,128)S(1)}, f32[8,128]{1,0:T(8,128)S(1)}, u32[]{:S(2)}, u32[]{:S(2)}) collective-permute-start(f32[8,128]{1,0:T(8,128)S(1)} %add_add_fusion.3), channel_id=1, source_target_pairs={{0,96},{8,104},{16,112},{24,120},{32,0},{40,8},{48,16},{56,24},{64... | collective-permute-start | bytes 12296 | tf_op jit(solution)/shard_map/ppermute | solution.py:40
  135.9 10.0 %collective-permute-start.44 = (bf16[288,768]{1,0:T(8,128)(2,1)S(1)}, bf16[288,768]{1,0:T(8,128)(2,1)S(1)}, u32[]{:S(2)}, u32[]{:S(2)}) collective-permute-start(bf16[288,768]{1,0:T(8,128)(2,1)S(1)} %get-tuple-element.155), channel_id=1, source_target_pairs={{32,0},{40,8},{48,16},{56,24},{64,32},{72,40},{80,48},{88,56},{96,... | collective-permute-start | bytes 1327112 | tf_op jit(solution)/shard_map/ppermute | solution.py:35
  139.0 10.3 %collective-permute-start.38 = (f16[96,768]{1,0:T(8,128)(2,1)S(1)}, f16[96,768]{1,0:T(8,128)(2,1)S(1)}, u32[]{:S(2)}, u32[]{:S(2)}) collective-permute-start(f16[96,768]{1,0:T(8,128)(2,1)S(1)} %get-tuple-element.170), channel_id=1, source_target_pairs={{0,24},{8,0},{16,8},{24,16},{32,56},{40,32},{48,40},{56,48},{64,88... | collective-permute-start | bytes 442376 | tf_op jit(solution)/shard_map/ppermute | solution.py:29
  140.4 9.7 %collective-permute-start.37 = (f16[96,768]{1,0:T(8,128)(2,1)S(1)}, f16[96,768]{1,0:T(8,128)(2,1)S(1)}, u32[]{:S(2)}, u32[]{:S(2)}) collective-permute-start(f16[96,768]{1,0:T(8,128)(2,1)S(1)} %get-tuple-element.171), channel_id=1, source_target_pairs={{0,16},{8,24},{16,0},{24,8},{32,48},{40,56},{48,32},{56,40},{64,80... | collective-permute-start | bytes 442376 | tf_op jit(solution)/shard_map/ppermute | solution.py:29
  147.6 10.5 %collective-permute-start.47 = (f16[96,768]{1,0:T(8,128)(2,1)S(1)}, f16[96,768]{1,0:T(8,128)(2,1)S(1)}, u32[]{:S(2)}, u32[]{:S(2)}) collective-permute-start(f16[96,768]{1,0:T(8,128)(2,1)S(1)} %get-tuple-element.166), channel_id=1, source_target_pairs={{0,24},{8,0},{16,8},{24,16},{32,56},{40,32},{48,40},{56,48},{64,88... | collective-permute-start | bytes 442376 | tf_op jit(solution)/shard_map/ppermute | solution.py:29
  148.4 9.7 %collective-permute-start.46 = (f16[96,768]{1,0:T(8,128)(2,1)S(1)}, f16[96,768]{1,0:T(8,128)(2,1)S(1)}, u32[]{:S(2)}, u32[]{:S(2)}) collective-permute-start(f16[96,768]{1,0:T(8,128)(2,1)S(1)} %get-tuple-element.167), channel_id=1, source_target_pairs={{0,16},{8,24},{16,0},{24,8},{32,48},{40,56},{48,32},{56,40},{64,80... | collective-permute-start | bytes 442376 | tf_op jit(solution)/shard_map/ppermute | solution.py:29
  152.5 12.0 %collective-permute-start.39 = (f16[4,48,768]{2,1,0:T(8,128)(2,1)S(1)}, f16[4,48,768]{2,1,0:T(8,128)(2,1)S(1)}, u32[]{:S(2)}, u32[]{:S(2)}) collective-permute-start(f16[4,48,768]{2,1,0:T(8,128)(2,1)S(1)} %convert_element_type.115), channel_id=1, source_target_pairs={{0,1},{1,0},{2,3},{3,2},{4,5},{5,4},{6,7},{7,6},{8,9},{9,8},{10,11... | collective-permute-start | bytes 884744 | tf_op jit(solution)/shard_map/ppermute | solution.py:53
  180.4 9.7 %collective-permute-start.52 = (f16[2,48,768]{2,1,0:T(8,128)(2,1)S(1)}, f16[2,48,768]{2,1,0:T(8,128)(2,1)S(1)}, u32[]{:S(2)}, u32[]{:S(2)}) collective-permute-start(f16[2,48,768]{2,1,0:T(8,128)(2,1)S(1)} %fusion.10), channel_id=1, source_target_pairs={{0,2},{1,3},{2,4},{3,5},{4,6},{5,7},{6,0},{7,1},{8,10},{9,11},{10,... | collective-permute-start | bytes 442376 | tf_op jit(solution)/shard_map/ppermute | solution.py:49
  (50 other events, 292.3 us)

commit v2 on v1

--- a/solution.py
+++ b/solution.py
@@ -369,8 +369,12 @@
     piece = piece * (power * gain * (bound / h_scale))
     piece = piece - (bound * gain * recurrence[1]) * own_rows(resid)
     piece = piece - (bound * recurrence[2]) * own_rows(psi)
-    resid, squares = share_bonds(piece.astype(F16), 1.0 / bound)
-    mean = of_lines(of_line(squares))[0, 0] / cells
+    piece = piece.astype(F16)
+    own = jnp.sum(jnp.square(piece.astype(F32) * (1.0 / bound)))
+    tile = of_lines(of_line(jnp.full((8, 128), own)))
+    resid, _ = share_bonds(piece, 1.0 / bound)
+    tile = combined([tile] + [along_y(tile, e) for e in range(1, SIDE)])
+    mean = (tile + other_core(tile))[0, 0] / cells
     vec_two = resid * (1.0 / jnp.sqrt(mean + EPS))
     return (vec_one[None], vec_two[None])
 

time: 214 us -> 225 us (1.051)
  starting transfers between devices: 96.1 us -> 116 us
  waiting for transfers between devices: 52.9 us -> 43.3 us
    ppermute x6, starting transfers between devices: 10.2 us -> 19.8 us  [around_z(): lax.ppermute(block, 'sector', [(i, (i + SIDE * step) % count) for i in ra...]
    ppermute x6 -> x7, starting transfers between devices: 22.2 us -> 29.4 us  [other_core(): return lax.ppermute(block, 'mpo', [(i, i ^ 1) for i in range(2 * SIDE)])]
    ppermute x12 -> x15, waiting for transfers between devices: 19.3 us -> 15.8 us  [along_y(): return lax.ppermute(block, 'mpo', route)]
    ppermute x30, waiting for transfers between devices: 17.7 us -> 14.7 us  [along_x(): return lax.ppermute(block, 'sector', route)]
    ppermute x12 -> x15, starting transfers between devices: 13.8 us -> 16.5 us  [along_y(): return lax.ppermute(block, 'mpo', route)]
    ppermute x6 -> x7, waiting for transfers between devices: 5.89 us -> 3.92 us  [other_core(): return lax.ppermute(block, 'mpo', [(i, i ^ 1) for i in range(2 * SIDE)])]
  transfers between devices with their start and end apart: 62 -> 66, of which waited for: 29 -> 25; matrix products, arithmetic and copies ran while one was open for 5% -> 5% of each run, Pallas kernels for 10% -> 10%
where the time goes in v2:
time: 225 us; the launch traced here: 222 us
  starting transfers between devices  116 us (52%)
  waiting for transfers between devices  43.3 us (19%)
  Pallas kernels  30.6 us (14%)
  other arithmetic  12 us (5%)
  local copies, waits for them, and re-layouts  11.6 us (5%)
  between operations  8.41 us (4%)
    ppermute x30, starting transfers between devices, along_x(): return lax.ppermute(block, 'sector', route)  32.6 us
    pallas_call x18, Pallas kernels, call(): pl.pallas_call(body, out_shape=shapes, in_specs=[in_smem] * len(smem) + [...  30.6 us
    ppermute x7, starting transfers between devices, other_core(): return lax.ppermute(block, 'mpo', [(i, i ^ 1) for i in range(2 * SIDE)])  29.4 us
    ppermute x6, starting transfers between devices, around_z(): lax.ppermute(block, 'sector', [(i, (i + SIDE * step) % count) for i in ra...  19.8 us
    ppermute x8, starting transfers between devices, along_z(): return lax.ppermute(block, 'sector', route)  17.6 us
    ppermute x15, starting transfers between devices, along_y(): return lax.ppermute(block, 'mpo', route)  16.5 us
    ppermute x15, waiting for transfers between devices, along_y(): return lax.ppermute(block, 'mpo', route)  15.8 us
    ppermute x30, waiting for transfers between devices, along_x(): return lax.ppermute(block, 'sector', route)  14.7 us
  transfers between devices with their start and end apart: 66, of which 25 were waited for; matrix products, arithmetic and copies ran while one was open for 5% of the time, Pallas kernels for 10%

profile of v2, /device:TPU:1, one launch (start us, length us, event | category | flops | bytes accessed | tf_op | source)
XLA Modules:
  0.0 221.9 jit_solution(8642746296969700952)
XLA Ops:
  4.1 3.0 %shard_map.95 = (bf16[112,768]{1,0:T(8,128)(2,1)S(1)}, bf16[112,768]{1,0:T(8,128)(2,1)}, bf16[112,768]{1,0:T(8,128)(2,1)S(1)}, bf16[112,768]{1,0:T(8,128)(2,1)S(1)}, f32[8,128]{1,0:T(8,128)S(1)}) custom-call(s32[3]{0:T(128)S(1)} %get-tuple-element.193.place, f32[768,768]{1,0:T(8,128)S(1)} %bitcast.128, f32[768,768]{1,0:T(8,128)S(1)} %bitcast.126), custom_call_target="tpu_custom_call" | custom-call | flops 1358954496 | bytes 5410816 | tf_op jit(solution)/shard_map/pallas_call | solution.py:68
  9.1 2.4 %collective-permute-start.1 = (bf16[112,768]{1,0:T(8,128)(2,1)S(1)}, bf16[112,768]{1,0:T(8,128)(2,1)S(1)}, u32[]{:S(2)}, u32[]{:S(2)}) collective-permute-start(bf16[112,768]{1,0:T(8,128)(2,1)S(1)} %get-tuple-element.86), channel_id=1, source_target_pairs={{0,16},{8,24},{16,0},{24,8},{32,48},{40,56},{48,32},{56,40},{64,80... | collective-permute-start | bytes 516104 | tf_op jit(solution)/shard_map/ppermute | solution.py:29
  19.9 3.6 %collective-permute-start.3 = (bf16[304,768]{1,0:T(8,128)(2,1)S(1)}, bf16[304,768]{1,0:T(8,128)(2,1)S(1)}, u32[]{:S(2)}, u32[]{:S(2)}) collective-permute-start(bf16[304,768]{1,0:T(8,128)(2,1)S(1)} %get-tuple-element.94), channel_id=1, source_target_pairs={{0,32},{8,40},{16,48},{24,56},{32,64},{40,72},{48,80},{56,88},{64,... | collective-permute-start | bytes 1400840 | tf_op jit(solution)/shard_map/ppermute | solution.py:35
  36.3 4.0 %collective-permute-start.12 = (bf16[288,768]{1,0:T(8,128)(2,1)}, bf16[288,768]{1,0:T(8,128)(2,1)S(1)}, u32[]{:S(2)}, u32[]{:S(2)}) collective-permute-start(bf16[288,768]{1,0:T(8,128)(2,1)} %get-tuple-element.113), channel_id=1, source_target_pairs={{0,32},{8,40},{16,48},{24,56},{32,64},{40,72},{48,80},{56,88},{64,... | collective-permute-start | bytes 1327112 | tf_op jit(solution)/shard_map/ppermute | solution.py:35
  47.3 3.8 %collective-permute-done.13.refs_5_ = bf16[288,768]{1,0:T(8,128)(2,1)S(1)} collective-permute-done((bf16[288,768]{1,0:T(8,128)(2,1)}, bf16[288,768]{1,0:T(8,128)(2,1)S(1)}, u32[]{:S(2)}, u32[]{:S(2)}) %collective-permute-start.13) | collective-permute-done | bytes 442400 | tf_op jit(solution)/shard_map/ppermute | solution.py:35
  58.7 4.7 %collective-permute-start.8 = (f16[4,48,768]{2,1,0:T(8,128)(2,1)S(1)}, f16[4,48,768]{2,1,0:T(8,128)(2,1)S(1)}, u32[]{:S(2)}, u32[]{:S(2)}) collective-permute-start(f16[4,48,768]{2,1,0:T(8,128)(2,1)S(1)} %convert_element_type.103), channel_id=1, source_target_pairs={{0,1},{1,0},{2,3},{3,2},{4,5},{5,4},{6,7},{7,6},{8,9},{9,8},{10,11... | collective-permute-start | bytes 884744 | tf_op jit(solution)/shard_map/ppermute | solution.py:53
  65.8 3.8 %collective-permute-start.17 = (f16[4,48,768]{2,1,0:T(8,128)(2,1)S(1)}, f16[4,48,768]{2,1,0:T(8,128)(2,1)S(1)}, u32[]{:S(2)}, u32[]{:S(2)}) collective-permute-start(f16[4,48,768]{2,1,0:T(8,128)(2,1)S(1)} %convert_element_type.107), channel_id=1, source_target_pairs={{0,1},{1,0},{2,3},{3,2},{4,5},{5,4},{6,7},{7,6},{8,9},{9,8},{10,11... | collective-permute-start | bytes 884744 | tf_op jit(solution)/shard_map/ppermute | solution.py:53
  79.4 2.4 %collective-permute-done.19 = f16[2,48,768]{2,1,0:T(8,128)(2,1)S(1)} collective-permute-done((f16[2,48,768]{2,1,0:T(8,128)(2,1)S(1)}, f16[2,48,768]{2,1,0:T(8,128)(2,1)S(1)}, u32[]{:S(2)}, u32[]{:S(2)}) %collective-permute-start.19) | collective-permute-done | bytes 147488 | tf_op jit(solution)/shard_map/ppermute | solution.py:49
  87.0 2.5 %collective-permute-done.22 = f16[2,48,768]{2,1,0:T(8,128)(2,1)S(1)} collective-permute-done((f16[2,48,768]{2,1,0:T(8,128)(2,1)S(1)}, f16[2,48,768]{2,1,0:T(8,128)(2,1)S(1)}, u32[]{:S(2)}, u32[]{:S(2)}) %collective-permute-start.22) | collective-permute-done | bytes 147488 | tf_op jit(solution)/shard_map/ppermute | solution.py:49
  92.0 3.1 %collective-permute-start.24 = (f16[4,2,48,768]{3,2,1,0:T(8,128)(2,1)S(1)}, f16[4,2,48,768]{3,2,1,0:T(8,128)(2,1)S(1)}, u32[]{:S(2)}, u32[]{:S(2)}) collective-permute-start(f16[4,2,48,768]{3,2,1,0:T(8,128)(2,1)S(1)} %get-tuple-element.173), channel_id=1, source_target_pairs={{0,1},{1,0},{2,3},{3,2},{4,5},{5,4},{6,7},{7,6},{8,9},{9,8},{10,11... | collective-permute-start | bytes 1769480 | tf_op jit(solution)/shard_map/ppermute | solution.py:53
  105.8 5.5 %collective-permute-done.31.refs_1_ = bf16[112,768]{1,0:T(8,128)(2,1)S(1)} collective-permute-done((bf16[112,768]{1,0:T(8,128)(2,1)S(1)}, bf16[112,768]{1,0:T(8,128)(2,1)S(1)}, u32[]{:S(2)}, u32[]{:S(2)}) %collective-permute-start.31) | collective-permute-done | bytes 172064 | tf_op jit(solution)/shard_map/ppermute | solution.py:29
  112.4 3.2 %collective-permute-start.34 = (bf16[304,768]{1,0:T(8,128)(2,1)S(1)}, bf16[304,768]{1,0:T(8,128)(2,1)S(1)}, u32[]{:S(2)}, u32[]{:S(2)}) collective-permute-start(bf16[304,768]{1,0:T(8,128)(2,1)S(1)} %get-tuple-element.129), channel_id=1, source_target_pairs={{0,32},{8,40},{16,48},{24,56},{32,64},{40,72},{48,80},{56,88},{64,... | collective-permute-start | bytes 1400840 | tf_op jit(solution)/shard_map/ppermute | solution.py:35
  116.8 2.8 %collective-permute-start.27 = (f32[8,128]{1,0:T(8,128)S(1)}, f32[8,128]{1,0:T(8,128)S(1)}, u32[]{:S(2)}, u32[]{:S(2)}) collective-permute-start(f32[8,128]{1,0:T(8,128)S(1)} %get-tuple-element.120.refs_0_), channel_id=1, source_target_pairs={{0,24},{8,0},{16,8},{24,16},{32,56},{40,32},{48,40},{56,48},{64,88... | collective-permute-start | bytes 12296 | tf_op jit(solution)/shard_map/ppermute | solution.py:29
  125.9 2.6 %collective-permute-start.30 = (f32[8,128]{1,0:T(8,128)S(1)}, f32[8,128]{1,0:T(8,128)S(1)}, u32[]{:S(2)}, u32[]{:S(2)}) collective-permute-start(f32[8,128]{1,0:T(8,128)S(1)} %add_add_fusion.4), channel_id=1, source_target_pairs={{0,96},{8,104},{16,112},{24,120},{32,0},{40,8},{48,16},{56,24},{64... | collective-permute-start | bytes 12296 | tf_op jit(solution)/shard_map/ppermute | solution.py:40
  130.1 3.4 %collective-permute-start.29 = (f32[8,128]{1,0:T(8,128)S(1)}, f32[8,128]{1,0:T(8,128)S(1)}, u32[]{:S(2)}, u32[]{:S(2)}) collective-permute-start(f32[8,128]{1,0:T(8,128)S(1)} %add_add_fusion.4), channel_id=1, source_target_pairs={{0,64},{8,72},{16,80},{24,88},{32,96},{40,104},{48,112},{56,120},{... | collective-permute-start | bytes 12296 | tf_op jit(solution)/shard_map/ppermute | solution.py:40
  133.5 9.8 %collective-permute-start.28 = (f32[8,128]{1,0:T(8,128)S(1)}, f32[8,128]{1,0:T(8,128)S(1)}, u32[]{:S(2)}, u32[]{:S(2)}) collective-permute-start(f32[8,128]{1,0:T(8,128)S(1)} %add_add_fusion.4), channel_id=1, source_target_pairs={{0,32},{8,40},{16,48},{24,56},{32,64},{40,72},{48,80},{56,88},{64,... | collective-permute-start | bytes 12296 | tf_op jit(solution)/shard_map/ppermute | solution.py:40
  151.6 4.2 %collective-permute-done.44.refs_5_ = bf16[288,768]{1,0:T(8,128)(2,1)S(1)} collective-permute-done((bf16[288,768]{1,0:T(8,128)(2,1)S(1)}, bf16[288,768]{1,0:T(8,128)(2,1)S(1)}, u32[]{:S(2)}, u32[]{:S(2)}) %collective-permute-start.44) | collective-permute-done | bytes 442400 | tf_op jit(solution)/shard_map/ppermute | solution.py:35
  162.3 5.6 %collective-permute-start.39 = (f16[4,48,768]{2,1,0:T(8,128)(2,1)S(1)}, f16[4,48,768]{2,1,0:T(8,128)(2,1)S(1)}, u32[]{:S(2)}, u32[]{:S(2)}) collective-permute-start(f16[4,48,768]{2,1,0:T(8,128)(2,1)S(1)} %convert_element_type.118), channel_id=1, source_target_pairs={{0,1},{1,0},{2,3},{3,2},{4,5},{5,4},{6,7},{7,6},{8,9},{9,8},{10,11... | collective-permute-start | bytes 884744 | tf_op jit(solution)/shard_map/ppermute | solution.py:53
  170.4 3.9 %collective-permute-start.48 = (f16[4,48,768]{2,1,0:T(8,128)(2,1)S(1)}, f16[4,48,768]{2,1,0:T(8,128)(2,1)S(1)}, u32[]{:S(2)}, u32[]{:S(2)}) collective-permute-start(f16[4,48,768]{2,1,0:T(8,128)(2,1)S(1)} %convert_element_type.122), channel_id=1, source_target_pairs={{0,1},{1,0},{2,3},{3,2},{4,5},{5,4},{6,7},{7,6},{8,9},{9,8},{10,11... | collective-permute-start | bytes 884744 | tf_op jit(solution)/shard_map/ppermute | solution.py:53
  176.4 2.7 %collective-permute-start.51 = (f16[2,48,768]{2,1,0:T(8,128)(2,1)}, f16[2,48,768]{2,1,0:T(8,128)(2,1)}, u32[]{:S(2)}, u32[]{:S(2)}) collective-permute-start(f16[2,48,768]{2,1,0:T(8,128)(2,1)} %get-tuple-element.163), channel_id=1, source_target_pairs={{0,6},{1,7},{2,0},{3,1},{4,2},{5,3},{6,4},{7,5},{8,14},{9,15},{10,... | collective-permute-start | bytes 442376 | tf_op jit(solution)/shard_map/ppermute | solution.py:49
  190.4 3.3 %collective-permute-start.54 = (f16[2,48,768]{2,1,0:T(8,128)(2,1)S(1)}, f16[2,48,768]{2,1,0:T(8,128)(2,1)S(1)}, u32[]{:S(2)}, u32[]{:S(2)}) collective-permute-start(f16[2,48,768]{2,1,0:T(8,128)(2,1)S(1)} %get-tuple-element.159), channel_id=1, source_target_pairs={{0,6},{1,7},{2,0},{3,1},{4,2},{5,3},{6,4},{7,5},{8,14},{9,15},{10,... | collective-permute-start | bytes 442376 | tf_op jit(solution)/shard_map/ppermute | solution.py:49
  201.4 3.3 %collective-permute-start.55 = (f16[4,2,48,768]{3,2,1,0:T(8,128)(2,1)S(1)}, f16[4,2,48,768]{3,2,1,0:T(8,128)(2,1)S(1)}, u32[]{:S(2)}, u32[]{:S(2)}) collective-permute-start(f16[4,2,48,768]{3,2,1,0:T(8,128)(2,1)S(1)} %get-tuple-element.160), channel_id=1, source_target_pairs={{0,1},{1,0},{2,3},{3,2},{4,5},{5,4},{6,7},{7,6},{8,9},{9,8},{10,11... | collective-permute-start | bytes 1769480 | tf_op jit(solution)/shard_map/ppermute | solution.py:53
  207.6 3.2 %collective-permute-done.63 = f32[8,128]{1,0:T(8,128)S(1)} collective-permute-done((f32[8,128]{1,0:T(8,128)S(1)}, f32[8,128]{1,0:T(8,128)S(1)}, u32[]{:S(2)}, u32[]{:S(2)}) %collective-permute-start.63) | collective-permute-done | bytes 4128 | tf_op jit(solution)/shard_map/ppermute | solution.py:49
  210.8 4.9 %collective-permute-start.65 = (f32[8,128]{1,0:T(8,128)S(1)}, f32[8,128]{1,0:T(8,128)S(1)}, u32[]{:S(2)}, u32[]{:S(2)}) collective-permute-start(f32[8,128]{1,0:T(8,128)S(1)} %add_add_fusion), channel_id=1, source_target_pairs={{0,1},{1,0},{2,3},{3,2},{4,5},{5,4},{6,7},{7,6},{8,9},{9,8},{10,11... | collective-permute-start | bytes 12296 | tf_op jit(solution)/shard_map/ppermute | solution.py:53
  (212 shorter events, 121.7 us)
Async XLA Ops:
  7.1 9.8 %collective-permute-start = (bf16[112,768]{1,0:T(8,128)(2,1)}, bf16[112,768]{1,0:T(8,128)(2,1)S(1)}, u32[]{:S(2)}, u32[]{:S(2)}) collective-permute-start(bf16[112,768]{1,0:T(8,128)(2,1)} %get-tuple-element.85), channel_id=1, source_target_pairs={{0,8},{8,16},{16,24},{24,0},{32,40},{40,48},{48,56},{56,32},{64,72... | collective-permute-start | bytes 516104 | tf_op jit(solution)/shard_map/ppermute | solution.py:29
  9.1 10.1 %collective-permute-start.1 = (bf16[112,768]{1,0:T(8,128)(2,1)S(1)}, bf16[112,768]{1,0:T(8,128)(2,1)S(1)}, u32[]{:S(2)}, u32[]{:S(2)}) collective-permute-start(bf16[112,768]{1,0:T(8,128)(2,1)S(1)} %get-tuple-element.86), channel_id=1, source_target_pairs={{0,16},{8,24},{16,0},{24,8},{32,48},{40,56},{48,32},{56,40},{64,80... | collective-permute-start | bytes 516104 | tf_op jit(solution)/shard_map/ppermute | solution.py:29
  19.9 16.3 %collective-permute-start.3 = (bf16[304,768]{1,0:T(8,128)(2,1)S(1)}, bf16[304,768]{1,0:T(8,128)(2,1)S(1)}, u32[]{:S(2)}, u32[]{:S(2)}) collective-permute-start(bf16[304,768]{1,0:T(8,128)(2,1)S(1)} %get-tuple-element.94), channel_id=1, source_target_pairs={{0,32},{8,40},{16,48},{24,56},{32,64},{40,72},{48,80},{56,88},{64,... | collective-permute-start | bytes 1400840 | tf_op jit(solution)/shard_map/ppermute | solution.py:35
  23.5 12.8 %collective-permute-start.4 = (bf16[304,768]{1,0:T(8,128)(2,1)S(1)}, bf16[304,768]{1,0:T(8,128)(2,1)S(1)}, u32[]{:S(2)}, u32[]{:S(2)}) collective-permute-start(bf16[304,768]{1,0:T(8,128)(2,1)S(1)} %get-tuple-element.95), channel_id=1, source_target_pairs={{32,0},{40,8},{48,16},{56,24},{64,32},{72,40},{80,48},{88,56},{96,... | collective-permute-start | bytes 1400840 | tf_op jit(solution)/shard_map/ppermute | solution.py:35
  36.3 11.0 %collective-permute-start.12 = (bf16[288,768]{1,0:T(8,128)(2,1)}, bf16[288,768]{1,0:T(8,128)(2,1)S(1)}, u32[]{:S(2)}, u32[]{:S(2)}) collective-permute-start(bf16[288,768]{1,0:T(8,128)(2,1)} %get-tuple-element.113), channel_id=1, source_target_pairs={{0,32},{8,40},{16,48},{24,56},{32,64},{40,72},{48,80},{56,88},{64,... | collective-permute-start | bytes 1327112 | tf_op jit(solution)/shard_map/ppermute | solution.py:35
  40.3 10.7 %collective-permute-start.13 = (bf16[288,768]{1,0:T(8,128)(2,1)}, bf16[288,768]{1,0:T(8,128)(2,1)S(1)}, u32[]{:S(2)}, u32[]{:S(2)}) collective-permute-start(bf16[288,768]{1,0:T(8,128)(2,1)} %get-tuple-element.114), channel_id=1, source_target_pairs={{32,0},{40,8},{48,16},{56,24},{64,32},{72,40},{80,48},{88,56},{96,... | collective-permute-start | bytes 1327112 | tf_op jit(solution)/shard_map/ppermute | solution.py:35
  43.7 11.7 %collective-permute-start.7 = (f16[96,768]{1,0:T(8,128)(2,1)S(1)}, f16[96,768]{1,0:T(8,128)(2,1)S(1)}, u32[]{:S(2)}, u32[]{:S(2)}) collective-permute-start(f16[96,768]{1,0:T(8,128)(2,1)S(1)} %get-tuple-element.183), channel_id=1, source_target_pairs={{0,24},{8,0},{16,8},{24,16},{32,56},{40,32},{48,40},{56,48},{64,88... | collective-permute-start | bytes 442376 | tf_op jit(solution)/shard_map/ppermute | solution.py:29
  45.7 10.5 %collective-permute-start.6 = (f16[96,768]{1,0:T(8,128)(2,1)S(1)}, f16[96,768]{1,0:T(8,128)(2,1)S(1)}, u32[]{:S(2)}, u32[]{:S(2)}) collective-permute-start(f16[96,768]{1,0:T(8,128)(2,1)S(1)} %get-tuple-element.184), channel_id=1, source_target_pairs={{0,16},{8,24},{16,0},{24,8},{32,48},{40,56},{48,32},{56,40},{64,80... | collective-permute-start | bytes 442376 | tf_op jit(solution)/shard_map/ppermute | solution.py:29
  46.1 10.1 %collective-permute-start.5 = (f16[96,768]{1,0:T(8,128)(2,1)S(1)}, f16[96,768]{1,0:T(8,128)(2,1)S(1)}, u32[]{:S(2)}, u32[]{:S(2)}) collective-permute-start(f16[96,768]{1,0:T(8,128)(2,1)S(1)} %get-tuple-element.185), channel_id=1, source_target_pairs={{0,8},{8,16},{16,24},{24,0},{32,40},{40,48},{48,56},{56,32},{64,72... | collective-permute-start | bytes 442376 | tf_op jit(solution)/shard_map/ppermute | solution.py:29
  52.7 10.7 %collective-permute-start.16 = (f16[96,768]{1,0:T(8,128)(2,1)S(1)}, f16[96,768]{1,0:T(8,128)(2,1)S(1)}, u32[]{:S(2)}, u32[]{:S(2)}) collective-permute-start(f16[96,768]{1,0:T(8,128)(2,1)S(1)} %get-tuple-element.179), channel_id=1, source_target_pairs={{0,24},{8,0},{16,8},{24,16},{32,56},{40,32},{48,40},{56,48},{64,88... | collective-permute-start | bytes 442376 | tf_op jit(solution)/shard_map/ppermute | solution.py:29
  58.7 11.0 %collective-permute-start.8 = (f16[4,48,768]{2,1,0:T(8,128)(2,1)S(1)}, f16[4,48,768]{2,1,0:T(8,128)(2,1)S(1)}, u32[]{:S(2)}, u32[]{:S(2)}) collective-permute-start(f16[4,48,768]{2,1,0:T(8,128)(2,1)S(1)} %convert_element_type.103), channel_id=1, source_target_pairs={{0,1},{1,0},{2,3},{3,2},{4,5},{5,4},{6,7},{7,6},{8,9},{9,8},{10,11... | collective-permute-start | bytes 884744 | tf_op jit(solution)/shard_map/ppermute | solution.py:53
  100.8 10.5 %collective-permute-start.31 = (bf16[112,768]{1,0:T(8,128)(2,1)S(1)}, bf16[112,768]{1,0:T(8,128)(2,1)S(1)}, u32[]{:S(2)}, u32[]{:S(2)}) collective-permute-start(bf16[112,768]{1,0:T(8,128)(2,1)S(1)} %get-tuple-element.122), channel_id=1, source_target_pairs={{0,8},{8,16},{16,24},{24,0},{32,40},{40,48},{48,56},{56,32},{64,72... | collective-permute-start | bytes 516104 | tf_op jit(solution)/shard_map/ppermute | solution.py:29
  100.9 10.5 %collective-permute-start.32 = (bf16[112,768]{1,0:T(8,128)(2,1)S(1)}, bf16[112,768]{1,0:T(8,128)(2,1)S(1)}, u32[]{:S(2)}, u32[]{:S(2)}) collective-permute-start(bf16[112,768]{1,0:T(8,128)(2,1)S(1)} %get-tuple-element.123), channel_id=1, source_target_pairs={{0,16},{8,24},{16,0},{24,8},{32,48},{40,56},{48,32},{56,40},{64,80... | collective-permute-start | bytes 516104 | tf_op jit(solution)/shard_map/ppermute | solution.py:29
  112.4 31.6 %collective-permute-start.34 = (bf16[304,768]{1,0:T(8,128)(2,1)S(1)}, bf16[304,768]{1,0:T(8,128)(2,1)S(1)}, u32[]{:S(2)}, u32[]{:S(2)}) collective-permute-start(bf16[304,768]{1,0:T(8,128)(2,1)S(1)} %get-tuple-element.129), channel_id=1, source_target_pairs={{0,32},{8,40},{16,48},{24,56},{32,64},{40,72},{48,80},{56,88},{64,... | collective-permute-start | bytes 1400840 | tf_op jit(solution)/shard_map/ppermute | solution.py:35
  115.5 28.5 %collective-permute-start.35 = (bf16[304,768]{1,0:T(8,128)(2,1)S(1)}, bf16[304,768]{1,0:T(8,128)(2,1)S(1)}, u32[]{:S(2)}, u32[]{:S(2)}) collective-permute-start(bf16[304,768]{1,0:T(8,128)(2,1)S(1)} %get-tuple-element.130), channel_id=1, source_target_pairs={{32,0},{40,8},{48,16},{56,24},{64,32},{72,40},{80,48},{88,56},{96,... | collective-permute-start | bytes 1400840 | tf_op jit(solution)/shard_map/ppermute | solution.py:35
  125.9 21.1 %collective-permute-start.30 = (f32[8,128]{1,0:T(8,128)S(1)}, f32[8,128]{1,0:T(8,128)S(1)}, u32[]{:S(2)}, u32[]{:S(2)}) collective-permute-start(f32[8,128]{1,0:T(8,128)S(1)} %add_add_fusion.4), channel_id=1, source_target_pairs={{0,96},{8,104},{16,112},{24,120},{32,0},{40,8},{48,16},{56,24},{64... | collective-permute-start | bytes 12296 | tf_op jit(solution)/shard_map/ppermute | solution.py:40
  130.1 16.9 %collective-permute-start.29 = (f32[8,128]{1,0:T(8,128)S(1)}, f32[8,128]{1,0:T(8,128)S(1)}, u32[]{:S(2)}, u32[]{:S(2)}) collective-permute-start(f32[8,128]{1,0:T(8,128)S(1)} %add_add_fusion.4), channel_id=1, source_target_pairs={{0,64},{8,72},{16,80},{24,88},{32,96},{40,104},{48,112},{56,120},{... | collective-permute-start | bytes 12296 | tf_op jit(solution)/shard_map/ppermute | solution.py:40
  133.5 13.5 %collective-permute-start.28 = (f32[8,128]{1,0:T(8,128)S(1)}, f32[8,128]{1,0:T(8,128)S(1)}, u32[]{:S(2)}, u32[]{:S(2)}) collective-permute-start(f32[8,128]{1,0:T(8,128)S(1)} %add_add_fusion.4), channel_id=1, source_target_pairs={{0,32},{8,40},{16,48},{24,56},{32,64},{40,72},{48,80},{56,88},{64,... | collective-permute-start | bytes 12296 | tf_op jit(solution)/shard_map/ppermute | solution.py:40
  145.7 10.1 %collective-permute-start.44 = (bf16[288,768]{1,0:T(8,128)(2,1)S(1)}, bf16[288,768]{1,0:T(8,128)(2,1)S(1)}, u32[]{:S(2)}, u32[]{:S(2)}) collective-permute-start(bf16[288,768]{1,0:T(8,128)(2,1)S(1)} %get-tuple-element.154), channel_id=1, source_target_pairs={{32,0},{40,8},{48,16},{56,24},{64,32},{72,40},{80,48},{88,56},{96,... | collective-permute-start | bytes 1327112 | tf_op jit(solution)/shard_map/ppermute | solution.py:35
  148.8 10.4 %collective-permute-start.38 = (f16[96,768]{1,0:T(8,128)(2,1)S(1)}, f16[96,768]{1,0:T(8,128)(2,1)S(1)}, u32[]{:S(2)}, u32[]{:S(2)}) collective-permute-start(f16[96,768]{1,0:T(8,128)(2,1)S(1)} %get-tuple-element.166), channel_id=1, source_target_pairs={{0,24},{8,0},{16,8},{24,16},{32,56},{40,32},{48,40},{56,48},{64,88... | collective-permute-start | bytes 442376 | tf_op jit(solution)/shard_map/ppermute | solution.py:29
  157.5 10.4 %collective-permute-start.47 = (f16[96,768]{1,0:T(8,128)(2,1)S(1)}, f16[96,768]{1,0:T(8,128)(2,1)S(1)}, u32[]{:S(2)}, u32[]{:S(2)}) collective-permute-start(f16[96,768]{1,0:T(8,128)(2,1)S(1)} %get-tuple-element.170), channel_id=1, source_target_pairs={{0,24},{8,0},{16,8},{24,16},{32,56},{40,32},{48,40},{56,48},{64,88... | collective-permute-start | bytes 442376 | tf_op jit(solution)/shard_map/ppermute | solution.py:29
  158.2 9.8 %collective-permute-start.46 = (f16[96,768]{1,0:T(8,128)(2,1)S(1)}, f16[96,768]{1,0:T(8,128)(2,1)S(1)}, u32[]{:S(2)}, u32[]{:S(2)}) collective-permute-start(f16[96,768]{1,0:T(8,128)(2,1)S(1)} %get-tuple-element.171), channel_id=1, source_target_pairs={{0,16},{8,24},{16,0},{24,8},{32,48},{40,56},{48,32},{56,40},{64,80... | collective-permute-start | bytes 442376 | tf_op jit(solution)/shard_map/ppermute | solution.py:29
  162.3 12.0 %collective-permute-start.39 = (f16[4,48,768]{2,1,0:T(8,128)(2,1)S(1)}, f16[4,48,768]{2,1,0:T(8,128)(2,1)S(1)}, u32[]{:S(2)}, u32[]{:S(2)}) collective-permute-start(f16[4,48,768]{2,1,0:T(8,128)(2,1)S(1)} %convert_element_type.118), channel_id=1, source_target_pairs={{0,1},{1,0},{2,3},{3,2},{4,5},{5,4},{6,7},{7,6},{8,9},{9,8},{10,11... | collective-permute-start | bytes 884744 | tf_op jit(solution)/shard_map/ppermute | solution.py:53
  201.4 17.1 %collective-permute-start.55 = (f16[4,2,48,768]{3,2,1,0:T(8,128)(2,1)S(1)}, f16[4,2,48,768]{3,2,1,0:T(8,128)(2,1)S(1)}, u32[]{:S(2)}, u32[]{:S(2)}) collective-permute-start(f16[4,2,48,768]{3,2,1,0:T(8,128)(2,1)S(1)} %get-tuple-element.160), channel_id=1, source_target_pairs={{0,1},{1,0},{2,3},{3,2},{4,5},{5,4},{6,7},{7,6},{8,9},{9,8},{10,11... | collective-permute-start | bytes 1769480 | tf_op jit(solution)/shard_map/ppermute | solution.py:53
  (54 other events, 339.4 us)
